TPU v7x, 256 devices: a whole 4x4x8 slice. The times are simulated.
256 devices in a mesh: dp: 64 (over z, y_lo, x), ctx: 4 (over y_hi, core).
Axes of the slice: x: 4, y: 4 (y_hi: 2, y_lo: 2; y = y_hi * 2 + y_lo), z: 8, core: 2. Of those that a mesh axis runs over, the one named last changes fastest.
Arguments:
- event_ids: int32 [192, 1024], P('dp', 'ctx'), may hold values from 0 to 2047
- lengths: int32 [192], P('dp'), may hold values from 128 to 1024, as said below
- event_side: bfloat16 [192, 1024, 512], P('dp', 'ctx'), may hold values from -4 to 4
- dense_input: bfloat16 [192, 1024], P('dp'), may hold values from -6 to 6
- labels: int32 [192, 2], P('dp'), may hold values 0 or 1
- event_table: bfloat16 [2048, 512], replicated, may hold values from -6 to 6
- seq_gain: float32 [512], replicated, may hold values from 0.1 to 1.9
- w_mix: bfloat16 [1024, 512], replicated, may hold values from -0.1875 to 0.1875
- w_query: bfloat16 [512, 512], replicated
- w_key: bfloat16 [512, 512], replicated
- w_value: bfloat16 [512, 512], replicated, may hold values from -0.25 to 0.25
- w_out: bfloat16 [512, 512], replicated, may hold values from -0.25 to 0.25
- w_pool: bfloat16 [512, 1024], replicated, may hold values from -0.25 to 0.25
- w_cross: bfloat16 [1024, 1024], replicated, may hold values from -0.1875 to 0.1875
- b_cross: float32 [1024], replicated, may hold values from -3 to 3
- w_heads: float32 [1024, 2], replicated, may hold values from -0.1875 to 0.1875
Outputs:
- grad_sequence: float32 [3072, 512], P(('dp', 'ctx'))
- grad_mix: float32 [1024, 512], P(('dp', 'ctx'))
- grad_cross: float32 [1024, 1024], P(('dp', 'ctx'))
- grad_gain: float32 [512], replicated
- grad_bias: float32 [1024], replicated
- grad_heads: float32 [1024, 2], replicated
Inputs may be any that keep to these rules, and one draw needn't show every extreme that they name: Sample b's history holds lengths[b] events in its first slots; the rest of its 1024 slots are padding.
All inputs are finite; a program needn't handle non-finite values. No bound on the sum of `labels` on one device may be relied on, other than what follows from the above.
Results may differ from a plain program's by a relative error of at most 0.015.
The roundings to bfloat16 on the way count: a program that leaves them out, or rounds other values in their place, can miss the bound.
Values may be sent and summed in bfloat16 or wider, within the bound.
No kernel may reach another device: no remote copies, remote signals or barrier semaphores. Data moves between devices by JAX's collectives and lax.ppermute only.
A program may use at most 192 MiB of HBM per device.

v0:
```python
import functools

import jax
import jax.numpy as jnp
from jax import lax
from jax.experimental import pallas as pl
from jax.experimental.pallas import tpu as pltpu
from jax.sharding import Mesh, PartitionSpec as P

HEADS = 8
BATCH = 192
SAMPLES = 3
BLOCK = 256
BLOCKS = 4
LEN = 1024
D = 512
DI = 1024
VOCAB = 2048
MASKED = -1e30
EPSILON = 1e-06
LOSS_SCALE = 32768.0
F32 = jnp.float32
BF16 = jnp.bfloat16
CTX = ("yhi", "core")
PLANE = ("ylo", "x", "yhi")


def dot(a, b):
    return lax.dot_general(a, b, (((1,), (0,)), ((), ())), preferred_element_type=F32)


def dot_nt(a, b):
    return lax.dot_general(a, b, (((1,), (1,)), ((), ())), preferred_element_type=F32)


def dot_tn(a, b):
    return lax.dot_general(a, b, (((0,), (0,)), ((), ())), preferred_element_type=F32)


def both_heads(rows):
    low = lax.broadcasted_iota(jnp.int32, rows.shape, 1) < 64
    zero = jnp.zeros_like(rows)
    return jnp.concatenate([jnp.where(low, rows, zero), jnp.where(low, zero, rows)], axis=0)


def causal(tile):
    key = lax.broadcasted_iota(jnp.int32, tile.shape, 0)
    query = lax.broadcasted_iota(jnp.int32, tile.shape, 1) & (BLOCK - 1)
    return key <= query


def spread(core, block_of, own_ref, other_ref):
    for mine in (0, 1):

        @pl.when(core == mine)
        def _():
            for quarter in range(4):
                target = own_ref if quarter // 2 == mine else other_ref
                lanes = slice(quarter * 128, (quarter + 1) * 128)
                for n in range(4):
                    for a in range(8):
                        start = n * 384 + a * 48
                        target[2 * a + quarter % 2, n * 48 : (n + 1) * 48, :] = block_of(start, lanes)


def forward_kernel(
    meta, part0, part1, part2, part3, mix_ref, gain_ref, base_ref, dense_ref, heads_ref,
    table_far, wq_far, wk_far, wv_far, wo_far, wp_far,
    q_ref, k_ref, v_ref, do_ref, mixed_ref, normed_ref, lse_ref, delta_ref, own_ref, other_ref,
    packet_ref, logit_ref,
    part_ref, q_all, k_all, vt_ref, att_ref, o_ref, res_ref, pre_ref, sum_ref, scaled_ref,
    term_acc, table_ref, wq_ref, wk_ref, wv_ref, wo_ref, wp_ref, sems,
):
    far = (table_far, wq_far, wk_far, wv_far, wo_far, wp_far)
    near = (table_ref, wq_ref, wk_ref, wv_ref, wo_ref, wp_ref)
    copies = [pltpu.make_async_copy(f, n, sems.at[i]) for i, (f, n) in enumerate(zip(far, near))]
    step = pl.program_id(0)
    length = meta[1]

    @pl.when(step == 0)
    def _():
        for copy in copies:
            copy.start()
        sum_ref[...] = jnp.zeros_like(sum_ref)
        term_acc[...] = jnp.zeros_like(term_acc)

    source = lax.rem(meta[0] - jnp.minimum(step, BLOCKS - 1) + BLOCKS, BLOCKS)
    for n, ref in enumerate((part0, part1, part2, part3)):

        @pl.when((step < BLOCKS) & (source == n))
        def _():
            part_ref[...] = ref[...]

    def ahead(c):
        here = slice(c * BLOCK, (c + 1) * BLOCK)
        if c == 0:
            for copy in copies[:4]:
                copy.wait()
        codes = part_ref[BLOCK:, :].astype(F32)
        ids = (codes[:, :BLOCK] * 256.0 + codes[:, BLOCK:]).T[:, 0:1].astype(jnp.int32)
        slots = lax.broadcasted_iota(jnp.int32, (BLOCK, VOCAB), 1)
        picked = jnp.where(slots == ids, 1.0, 0.0).astype(BF16)
        tokens = dot(picked, table_ref[...]) + part_ref[:BLOCK, :].astype(F32)
        mean = jnp.mean(tokens * tokens, axis=1, keepdims=True)
        normed = tokens * lax.rsqrt(mean + EPSILON)
        normed_ref[...] = normed.astype(BF16)
        mixed = (normed * gain_ref[...] + mix_ref[...]).astype(BF16)
        mixed_ref[...] = mixed
        queries = (dot(mixed, wq_ref[...]).astype(BF16).astype(F32) * 0.125).astype(BF16)
        q_ref[...] = queries
        q_all[...] = queries
        keys_now = dot(mixed, wk_ref[...]).astype(BF16)
        k_ref[...] = keys_now
        k_all[here, :] = keys_now
        values = dot(mixed, wv_ref[...]).astype(BF16)
        v_ref[...] = values
        vt_ref[:, here] = values.T
        for p in range(4):
            lanes = slice(p * 128, (p + 1) * 128)
            chosen = both_heads(q_all[:, lanes])
            tiles = []
            for j in range(c + 1):
                tile = dot_nt(k_all[j * BLOCK : (j + 1) * BLOCK, lanes], chosen)
                if j == c:
                    tile = jnp.where(causal(tile), tile, MASKED)
                tiles.append(tile)
            top = functools.reduce(jnp.maximum, [jnp.max(t, axis=0, keepdims=True) for t in tiles])
            raised = [jnp.exp(t - top) for t in tiles]
            total = functools.reduce(jnp.add, [jnp.sum(t, axis=0, keepdims=True) for t in raised])
            inverse = 1.0 / total
            shares = [(t * inverse).astype(BF16) for t in raised]
            lse = top + jnp.log(total)
            lse_ref[p, 0:1, here] = lse[:, :BLOCK]
            lse_ref[p, 1:2, here] = lse[:, BLOCK:]
            first = jnp.zeros((64, BLOCK), F32)
            second = jnp.zeros((64, BLOCK), F32)
            for j in range(c + 1):
                keys = slice(j * BLOCK, (j + 1) * BLOCK)
                first += dot(vt_ref[p * 128 : p * 128 + 64, keys], shares[j][:, :BLOCK])
                second += dot(vt_ref[p * 128 + 64 : p * 128 + 128, keys], shares[j][:, BLOCK:])
            joined = jnp.concatenate([first, second], axis=0).T
            o_ref[here, lanes] = joined
            att_ref[here, lanes] = joined.astype(BF16)
        if c == 0:
            for copy in copies[4:]:
                copy.wait()
        residual = tokens + dot(att_ref[here, :], wo_ref[...])
        half = residual.astype(BF16)
        res_ref[here, :] = half
        pre = dot(half, wp_ref[...])
        pre_ref[here, :] = pre
        valid = (c * BLOCK + lax.broadcasted_iota(jnp.int32, pre.shape, 0)) < length
        silu = jnp.where(valid, pre * jax.nn.sigmoid(pre), 0.0)
        sum_ref[...] += jnp.sum(silu, axis=0, keepdims=True)

    def blank(c):
        if c == 0:
            for copy in copies:
                copy.wait()
        here = slice(c * BLOCK, (c + 1) * BLOCK)
        for ref in (q_ref, k_ref, v_ref, mixed_ref, normed_ref):
            ref[...] = jnp.zeros((BLOCK, D), ref.dtype)
        lse_ref[:, :, here] = jnp.zeros((4, 2, BLOCK), F32)
        delta_ref[:, :, here] = jnp.zeros((4, 2, BLOCK), F32)

    for c in range(BLOCKS):
        pl.when((step == c) & (length > c * BLOCK))(functools.partial(ahead, c))
        pl.when((step == c) & (length <= c * BLOCK))(functools.partial(blank, c))

    @pl.when(step == BLOCKS)
    def _():
        span = jnp.maximum(length, 1).astype(F32)
        dense = dense_ref[...]
        gate = base_ref[...] + sum_ref[...] / span
        crossed = dense + dense * gate
        rows = [dense[:, n * 128 : (n + 1) * 128] for n in range(8)]
        rows += [crossed[:, n * 128 : (n + 1) * 128] for n in range(8)]
        packet_ref[...] = jnp.concatenate(rows, axis=0).astype(BF16)
        a = jnp.sum(crossed * heads_ref[0:1, :], axis=1, keepdims=True)
        c = jnp.sum(crossed * heads_ref[1:2, :], axis=1, keepdims=True)
        clicked = meta[2].astype(F32)
        converted = (meta[2] * meta[3]).astype(F32)
        top = jnp.maximum(jnp.maximum(a, c), 0.0)
        ea, ec = jnp.exp(a - top), jnp.exp(c - top)
        below = jnp.exp(-top) + ea + ec
        grad_a = jax.nn.sigmoid(a) - clicked - converted * jax.nn.sigmoid(-a)
        grad_a = grad_a - (1.0 - converted) * (ea / below - jax.nn.sigmoid(a))
        grad_c = -converted * jax.nn.sigmoid(-c)
        grad_c = grad_c - (1.0 - converted) * (ec / below - jax.nn.sigmoid(c))
        factor = jnp.where(length > 0, LOSS_SCALE / BATCH, 0.0)
        grad_a = grad_a * factor
        grad_c = grad_c * factor
        lane = lax.broadcasted_iota(jnp.int32, (1, 128), 1)
        logit_ref[...] = jnp.where(lane == 0, grad_a, jnp.where(lane == 1, grad_c, 0.0))
        grad_gate = (grad_a * heads_ref[0:1, :] + grad_c * heads_ref[1:2, :]) * dense
        scaled_ref[...] = grad_gate / span

    def back(c):
        here = slice(c * BLOCK, (c + 1) * BLOCK)
        pre = pre_ref[here, :]
        sig = jax.nn.sigmoid(pre)
        valid = (c * BLOCK + lax.broadcasted_iota(jnp.int32, pre.shape, 0)) < length
        slope = sig * (1.0 + pre * (1.0 - sig)) * scaled_ref[...]
        grad_pre = jnp.where(valid, slope, 0.0).astype(BF16)
        term_acc[D:, :] += dot_tn(grad_pre, res_ref[here, :])
        grad_res = dot_nt(grad_pre, wp_ref[...]).astype(BF16)
        term_acc[:D, :] += dot_tn(att_ref[here, :], grad_res)
        grad_att = dot_nt(grad_res, wo_ref[...]).astype(BF16)
        do_ref[...] = grad_att
        product = grad_att.astype(F32) * o_ref[here, :]
        head = lax.broadcasted_iota(jnp.int32, (HEADS, D), 0)
        column = lax.broadcasted_iota(jnp.int32, (HEADS, D), 1) // 64
        picks = jnp.where(head == column, 1.0, 0.0).astype(BF16)
        high = product.astype(BF16)
        low = (product - high.astype(F32)).astype(BF16)
        delta = dot_nt(picks, high) + dot_nt(picks, low)
        for p in range(4):
            delta_ref[p, :, here] = delta[2 * p : 2 * p + 2, :]

    def quiet():
        do_ref[...] = jnp.zeros((BLOCK, D), BF16)

    for c in range(BLOCKS):
        pl.when((step == BLOCKS + c) & (length > c * BLOCK))(functools.partial(back, c))
        pl.when((step == BLOCKS + c) & (length <= c * BLOCK))(quiet)

    @pl.when(step == 2 * BLOCKS - 1)
    def _():
        spread(
            meta[6], lambda row, lanes: term_acc[row : row + 48, lanes].astype(BF16), own_ref, other_ref
        )


def pair_body(
    length, q_ref, k_ref, v_ref, do_ref, lse_ref, delta_ref, dq_ref, dk_ref, dv_ref, dk_acc, dv_acc, kt_ref
):
    dk_acc[...] = jnp.zeros_like(dk_acc)
    dv_acc[...] = jnp.zeros_like(dv_acc)
    kt_ref[...] = k_ref[...].T

    def block(c):
        here = slice(c * BLOCK, (c + 1) * BLOCK)
        chosen = both_heads(q_ref[here, :])
        grads = both_heads(do_ref[here, :])
        lse = jnp.concatenate([lse_ref[0, 0:1, here], lse_ref[0, 1:2, here]], axis=1)
        delta = jnp.concatenate([delta_ref[0, 0:1, here], delta_ref[0, 1:2, here]], axis=1)
        first = jnp.zeros((64, BLOCK), F32)
        second = jnp.zeros((64, BLOCK), F32)
        for j in range(c + 1):
            keys = slice(j * BLOCK, (j + 1) * BLOCK)
            shares = jnp.exp(dot_nt(k_ref[keys, :], chosen) - lse)
            if j == c:
                shares = jnp.where(causal(shares), shares, 0.0)
            grad_shares = dot_nt(v_ref[keys, :], grads)
            grad_scores = (shares * (grad_shares - delta)).astype(BF16)
            dv_acc[keys, :] += dot(shares.astype(BF16), grads)
            dk_acc[keys, :] += dot(grad_scores, chosen)
            first += dot(kt_ref[0:64, keys], grad_scores[:, :BLOCK])
            second += dot(kt_ref[64:128, keys], grad_scores[:, BLOCK:])
        joined = jnp.concatenate([first, second], axis=0) * 0.125
        dq_ref[here, :] = joined.T.astype(BF16)

    def blank(c):
        here = slice(c * BLOCK, (c + 1) * BLOCK)
        dq_ref[here, :] = jnp.zeros((BLOCK, 128), BF16)

    for c in range(BLOCKS):
        pl.when(length > c * BLOCK)(functools.partial(block, c))
        pl.when(length <= c * BLOCK)(functools.partial(blank, c))
    dk_ref[...] = dk_acc[...].astype(BF16)
    dv_ref[...] = dv_acc[...].astype(BF16)


def pair_kernel(
    meta, q_ref, k_ref, v_ref, do_ref, lse_ref, delta_ref, grad_ref, dk_acc, dv_acc, kt_ref
):
    pair_body(
        meta[1], q_ref, k_ref, v_ref, do_ref, lse_ref, delta_ref,
        grad_ref.at[0], grad_ref.at[1], grad_ref.at[2], dk_acc, dv_acc, kt_ref,
    )


def rest_kernel(
    meta, q_ref, k_ref, v_ref, do_ref, lse_ref, delta_ref, logit_ref,
    one_far, mixed_far, normed_far, wq_far, wk_far, wv_far,
    own_ref, other_ref, packet_ref,
    dk_acc, dv_acc, kt_ref, term_ref, grad_ref, one_ref, mixed_ref, normed_ref, wq_ref, wk_ref, wv_ref, sems,
):
    step = pl.program_id(0)
    far = (one_far, mixed_far, normed_far, wq_far, wk_far, wv_far)
    near = (one_ref, mixed_ref, normed_ref, wq_ref, wk_ref, wv_ref)
    copies = [pltpu.make_async_copy(f, n, sems.at[i]) for i, (f, n) in enumerate(zip(far, near))]

    @pl.when(step == 0)
    def _():
        for copy in copies:
            copy.start()

    pair_body(
        meta[1], q_ref, k_ref, v_ref, do_ref, lse_ref, delta_ref,
        grad_ref.at[0, step], grad_ref.at[1, step], grad_ref.at[2, step], dk_acc, dv_acc, kt_ref,
    )

    @pl.when(step == 2)
    def _():
        for copy in copies:
            copy.wait()
        turned = mixed_ref[...].T
        total = None
        for n, weight in enumerate((wq_ref, wk_ref, wv_ref)):
            rows = jnp.concatenate([one_ref[n]] + [grad_ref[n, p] for p in range(3)], axis=1)
            term_ref[n * D : (n + 1) * D, :] = dot(turned, rows).astype(BF16)
            part = dot_nt(rows, weight[...])
            total = part if total is None else total + part
        spread(meta[6], lambda row, lanes: term_ref[row : row + 48, lanes], own_ref, other_ref)
        mix = jnp.sum(total, axis=0, keepdims=True)
        gain = jnp.sum(total * normed_ref[...].astype(F32), axis=0, keepdims=True)
        logit = logit_ref[...]
        high = logit.astype(BF16).astype(F32)
        lines = [mix[:, n * 128 : (n + 1) * 128] for n in range(4)]
        lines += [gain[:, n * 128 : (n + 1) * 128] for n in range(4)]
        lines += [high, logit - high, jnp.zeros((6, 128), F32)]
        packet_ref[...] = jnp.concatenate(lines, axis=0).astype(BF16)


def piece_kernel(own_ref, got_ref, packet_ref, piece_ref):
    for g in range(16):
        total = own_ref[g].astype(F32) + got_ref[g].astype(F32)
        piece_ref[g, :192, :] = total.astype(BF16)
        piece_ref[g, 192:, :] = packet_ref[...]


def exact_dot(a, b):
    return lax.dot_general(
        a, b, (((1,), (0,)), ((), ())),
        precision=lax.Precision.HIGHEST, preferred_element_type=F32,
    )


def sum_kernel(meta, upper_ref, lower_ref, heads_ref, piece_ref):
    upper_packets = [upper_ref[g, 192:, :].astype(F32) for g in range(16)]
    lower_packets = [lower_ref[g, 192:, :].astype(F32) for g in range(16)]

    def pick(packets, row):
        return jnp.concatenate([p[row : row + 1, :] for p in packets], axis=0)

    upper = functools.reduce(jnp.add, [upper_ref[g, :192, :].astype(F32) for g in range(16)])
    lower = functools.reduce(jnp.add, [lower_ref[g, :192, :].astype(F32) for g in range(16)])
    for n in range(4):
        piece_ref[n, :48, :] = lower[n * 48 : (n + 1) * 48].astype(BF16)
        piece_ref[4 + n, :48, :] = upper[n * 48 : (n + 1) * 48].astype(BF16)
    logits = pick(lower_packets, 8) + pick(lower_packets, 9)
    grad_a, grad_c = logits[:, 0:1], logits[:, 1:2]
    lane = lax.broadcasted_iota(jnp.int32, (8, 128), 1)
    line = lax.broadcasted_iota(jnp.int32, (8, 128), 0)
    picks = jnp.where(lane == meta[7] * 8 + line, 1.0, 0.0).astype(BF16)
    dense = [pick(upper_packets, r) for r in range(8)]
    columns = jnp.concatenate([dot_nt(picks, d.astype(BF16)) for d in dense], axis=0)
    flat = [jnp.sum(pick(lower_packets, 4 + r), axis=0, keepdims=True) for r in range(4)]
    gates = []
    for r in range(8):
        lanes = slice(r * 128, (r + 1) * 128)
        gate = (grad_a * heads_ref[0:1, lanes] + grad_c * heads_ref[1:2, lanes]) * dense[r]
        gates.append(gate)
        flat.append(jnp.sum(gate, axis=0, keepdims=True))
    crossed = [pick(upper_packets, 8 + r) for r in range(8)]
    flat += [jnp.sum(d * grad_a, axis=0, keepdims=True) for d in crossed]
    flat += [jnp.sum(d * grad_c, axis=0, keepdims=True) for d in crossed]
    flat = jnp.concatenate(flat + [jnp.zeros((4, 128), F32)], axis=0).astype(BF16)
    products = [exact_dot(columns, gate) for gate in gates]
    products += [exact_dot(columns, pick(lower_packets, r)) for r in range(4)]
    for z in range(8):
        rows = jnp.concatenate([p[z * 8 : (z + 1) * 8, :] for p in products], axis=0)
        piece_ref[z, 48:144, :] = rows.astype(BF16)
        piece_ref[z, 144:176, :] = flat


def final_kernel(meta, got_ref, row0, row1, row2, row3, share_ref):
    total = functools.reduce(jnp.add, [got_ref[z].astype(F32) for z in range(8)])
    for n in range(4):
        for k, ref in enumerate((row0, row1, row2, row3)):

            @pl.when(lax.rem(meta[0] + k, 4) == n)
            def _():
                ref[...] = total[n * 12 : (n + 1) * 12, :]

    share_ref[...] = total[48:176, :]


def join_kernel(meta, row0, row1, row2, row3, share_ref, swapped_ref, sequence_ref, mix_ref, cross_ref, gain_ref, bias_ref, heads_ref):
    for source, place in ((0, 0), (2, 1), (1, 2), (3, 3)):
        entry = lax.rem(meta[0] - source + 4, 4)
        for n, ref in enumerate((row0, row1, row2, row3)):

            @pl.when(entry == n)
            def _():
                sequence_ref[:, place * 128 : (place + 1) * 128] = ref[...]

    total = share_ref[...] + swapped_ref[...]
    upper = meta[6] == 1
    for r in range(12):
        mine = jnp.where(upper, total[r * 8 + 4 : r * 8 + 8, :], total[r * 8 : r * 8 + 4, :])
        if r < 8:
            cross_ref[:, r * 128 : (r + 1) * 128] = mine
        else:
            mix_ref[:, (r - 8) * 128 : (r - 7) * 128] = mine
    for r in range(4):
        gain_ref[:, r * 128 : (r + 1) * 128] = total[96 + r : 97 + r, :]
    for r in range(8):
        lanes = slice(r * 128, (r + 1) * 128)
        bias_ref[:, lanes] = total[100 + r : 101 + r, :]
        heads_ref[0:1, lanes] = total[108 + r : 109 + r, :]
        heads_ref[1:2, lanes] = total[116 + r : 117 + r, :]


def whole(shape):
    return pl.BlockSpec(shape, lambda i, m: (0,) * len(shape))


def params(megabytes):
    return pltpu.CompilerParams(
        dimension_semantics=("arbitrary",), vmem_limit_bytes=megabytes * 2**20
    )


def cost(flops, moved, exps=0):
    return pl.CostEstimate(flops=flops, bytes_accessed=moved, transcendentals=exps)


def forward(meta, small, large):
    early = pl.BlockSpec((BLOCK, D), lambda i, m: (jnp.minimum(i, BLOCKS - 1), 0))
    late = pl.BlockSpec((BLOCK, D), lambda i, m: (jnp.maximum(i - BLOCKS, 0), 0))
    outs = [((LEN, D), BF16)] * 6 + [
        ((4, 2, LEN), F32), ((4, 2, LEN), F32), ((16, 192, 128), BF16), ((16, 192, 128), BF16),
        ((16, 128), BF16),
        ((1, 128), F32),
    ]
    return pl.pallas_call(
        forward_kernel,
        grid_spec=pltpu.PrefetchScalarGridSpec(
            num_scalar_prefetch=1,
            grid=(2 * BLOCKS,),
            in_specs=[whole(a.shape) for a in small] + [pl.BlockSpec(memory_space=pl.ANY)] * 6,
            out_specs=[early] * 3 + [late] + [early] * 2 + [whole(s) for s, _ in outs[6:]],
            scratch_shapes=[
                pltpu.VMEM((BLOCK + 16, D), BF16),
                pltpu.VMEM((BLOCK, D), BF16),
                pltpu.VMEM((LEN, D), BF16),
                pltpu.VMEM((D, LEN), BF16),
                pltpu.VMEM((LEN, D), BF16),
                pltpu.VMEM((LEN, D), F32),
                pltpu.VMEM((LEN, D), BF16),
                pltpu.VMEM((LEN, DI), F32),
                pltpu.VMEM((1, DI), F32),
                pltpu.VMEM((1, DI), F32),
                pltpu.VMEM((3 * D, D), F32),
            ] + [pltpu.VMEM(a.shape, BF16) for a in large] + [pltpu.SemaphoreType.DMA((6,))],
        ),
        out_shape=[jax.ShapeDtypeStruct(s, t) for s, t in outs],
        compiler_params=params(58),
        cost_estimate=cost(10**10, 2 * 10**7, 10**7),
    )(meta, *small, *large)


def first_pair_back(meta, queries, keys, values, grads, lse, delta):
    lanes = pl.BlockSpec((LEN, 128), lambda i, m: (0, i))
    pair = pl.BlockSpec((1, 2, LEN), lambda i, m: (i, 0, 0))
    return pl.pallas_call(
        pair_kernel,
        grid_spec=pltpu.PrefetchScalarGridSpec(
            num_scalar_prefetch=1,
            grid=(1,),
            in_specs=[lanes] * 4 + [pair] * 2,
            out_specs=whole((3, LEN, 128)),
            scratch_shapes=[
                pltpu.VMEM((LEN, 128), F32),
                pltpu.VMEM((LEN, 128), F32),
                pltpu.VMEM((128, LEN), BF16),
            ],
        ),
        out_shape=jax.ShapeDtypeStruct((3, LEN, 128), BF16),
        compiler_params=params(60),
        cost_estimate=cost(4 * 10**9, 2 * 10**6, 2 * 10**6),
    )(meta, queries, keys, values, grads, lse, delta)


def rest_back(meta, queries, keys, values, grads, lse, delta, logit, *far):
    lanes = pl.BlockSpec((LEN, 128), lambda i, m: (0, 1 + i))
    pair = pl.BlockSpec((1, 2, LEN), lambda i, m: (1 + i, 0, 0))
    outs = ((16, 192, 128), (16, 192, 128), (16, 128))
    return pl.pallas_call(
        rest_kernel,
        grid_spec=pltpu.PrefetchScalarGridSpec(
            num_scalar_prefetch=1,
            grid=(3,),
            in_specs=[lanes] * 4 + [pair] * 2 + [whole(logit.shape)]
            + [pl.BlockSpec(memory_space=pl.ANY)] * 6,
            out_specs=[whole(s) for s in outs],
            scratch_shapes=[
                pltpu.VMEM((LEN, 128), F32),
                pltpu.VMEM((LEN, 128), F32),
                pltpu.VMEM((128, LEN), BF16),
                pltpu.VMEM((3 * D, D), BF16),
                pltpu.VMEM((3, 3, LEN, 128), BF16),
            ] + [pltpu.VMEM(a.shape, BF16) for a in far] + [pltpu.SemaphoreType.DMA((6,))],
        ),
        out_shape=[jax.ShapeDtypeStruct(s, BF16) for s in outs],
        compiler_params=params(60),
        cost_estimate=cost(16 * 10**9, 10**7, 6 * 10**6),
    )(meta, queries, keys, values, grads, lse, delta, logit, *far)


def cut_pieces(own, got, packet):
    return pl.pallas_call(
        piece_kernel,
        out_shape=jax.ShapeDtypeStruct((16, 208, 128), BF16),
        compiler_params=pltpu.CompilerParams(vmem_limit_bytes=16 * 2**20),
        cost_estimate=cost(10**6, 3 * 10**6),
    )(own, got, packet)


def sum_pieces(meta, upper, lower, heads):
    return pl.pallas_call(
        sum_kernel,
        grid_spec=pltpu.PrefetchScalarGridSpec(
            num_scalar_prefetch=1,
            grid=(1,),
            in_specs=[whole(a.shape) for a in (upper, lower, heads)],
            out_specs=whole((8, 176, 128)),
        ),
        out_shape=jax.ShapeDtypeStruct((8, 176, 128), BF16),
        compiler_params=params(16),
        cost_estimate=cost(10**7, 2 * 10**6),
    )(meta, upper, lower, heads)


def total_rows(meta, got):
    outs = ((12, 128),) * 4 + ((128, 128),)
    return pl.pallas_call(
        final_kernel,
        grid_spec=pltpu.PrefetchScalarGridSpec(
            num_scalar_prefetch=1,
            grid=(1,),
            in_specs=[whole(got.shape)],
            out_specs=[whole(s) for s in outs],
        ),
        out_shape=[jax.ShapeDtypeStruct(s, F32) for s in outs],
        compiler_params=params(16),
        cost_estimate=cost(10**6, 10**6),
    )(meta, got)


def join(meta, rows, share, swapped):
    outs = ((12, D), (4, D), (4, DI), (1, D), (1, DI), (2, DI))
    args = (*rows, share, swapped)
    return pl.pallas_call(
        join_kernel,
        grid_spec=pltpu.PrefetchScalarGridSpec(
            num_scalar_prefetch=1,
            grid=(1,),
            in_specs=[whole(a.shape) for a in args],
            out_specs=[whole(s) for s in outs],
        ),
        out_shape=[jax.ShapeDtypeStruct(s, F32) for s in outs],
        compiler_params=params(16),
        cost_estimate=cost(10**5, 10**5),
    )(meta, *args)


def to_samples(event_ids, event_side, me):
    codes = jnp.concatenate([event_ids // 256, event_ids % 256], axis=1).astype(BF16)
    codes = jnp.concatenate([codes[:, None], jnp.zeros((SAMPLES, 15, D), BF16)], axis=1)

    def part(sample):
        sample = jnp.minimum(sample, SAMPLES - 1)
        side = lax.dynamic_index_in_dim(event_side, sample, 0, keepdims=False)
        code = lax.dynamic_index_in_dim(codes, sample, 0, keepdims=False)
        return jnp.concatenate([side, code])

    got = [part(me)]
    for k in (1, 2, 3):
        pairs = [(i, (i + k) % 4) for i in range(4) if (i + k) % 4 < SAMPLES]
        got.append(lax.ppermute(part((me + k) % 4), CTX, pairs))
    return got


def swap_cores(value):
    return lax.ppermute(value, "core", [(0, 1), (1, 0)])


def per_device(
    event_ids, lengths, event_side, dense_input, labels, event_table, seq_gain, w_mix, w_query,
    w_key, w_value, w_out, w_pool, w_cross, b_cross, w_heads,
):
    me = lax.axis_index(CTX)
    core = lax.axis_index("core")
    chip = lax.axis_index(("z", "ylo", "x", "yhi"))
    own = jnp.minimum(me, SAMPLES - 1)
    parts = to_samples(event_ids, event_side, me)
    length = jnp.where(me < SAMPLES, lengths[own], 0)
    plane = lax.axis_index(PLANE)
    meta = [me, length, labels[own, 0], labels[own, 1], chip, lax.axis_index("z"), core, plane]
    meta = jnp.stack(meta).astype(jnp.int32)
    dense = lax.dynamic_slice_in_dim(dense_input, own, 1, 0)
    mix_row = dot(dense, w_mix)
    base = dot(dense, w_cross) + b_cross[None]

    heads = w_heads.T
    (queries, keys, values, grads, mixed, normed, lse, delta, own, other, packet, logit) = forward(
        meta,
        (*parts, mix_row, seq_gain[None], base, dense.astype(F32), heads),
        (event_table, w_query, w_key, w_value, w_out, w_pool),
    )
    upper_got = swap_cores(other)
    attention = (queries, keys, values, grads, lse, delta)
    one = first_pair_back(meta, *attention)
    upper_got, one = lax.optimization_barrier((upper_got, one))
    pieces = cut_pieces(own, upper_got, packet)
    pieces, attention = lax.optimization_barrier((pieces, attention))
    upper_plane = lax.all_to_all(pieces, PLANE, 0, 0)
    own, other, packet = rest_back(
        meta, *attention, logit, one, mixed, normed, w_query, w_key, w_value
    )
    upper_plane, other = lax.optimization_barrier((upper_plane, other))
    lower_got = swap_cores(other)
    pieces = cut_pieces(own, lower_got, packet)
    lower_plane = lax.all_to_all(pieces, PLANE, 0, 0)
    got = lax.all_to_all(sum_pieces(meta, upper_plane, lower_plane, heads), "z", 0, 0)
    *rows, share = total_rows(meta, got)
    entries = rows[:1]
    for k in (1, 2, 3):
        entries.append(lax.ppermute(rows[k], CTX, [(i, (i + k) % 4) for i in range(4)]))
    swapped = swap_cores(share)
    sequence, mix, cross, gain, bias, grad_heads = join(meta, entries, share, swapped)
    return (sequence, mix, cross, gain.reshape(D), bias.reshape(DI), grad_heads.T)


def solution(mesh):
    fine = Mesh(mesh.devices.reshape(8, 2, 4, 2, 2), ("z", "ylo", "x", "yhi", "core"))
    dp = ("z", "ylo", "x")
    every = dp + CTX
    in_specs = (P(dp, CTX), P(dp), P(dp, CTX, None), P(dp, None), P(dp, None)) + (P(),) * 11
    out_specs = (P(every, None), P(every, None), P(every, None), P(), P(), P())
    return jax.shard_map(
        per_device, mesh=fine, in_specs=in_specs, out_specs=out_specs, check_vma=False
    )
```

profile of v0, /device:TPU:1, one launch (start us, length us, event | category | flops | bytes accessed | tf_op | source)
XLA Modules:
  0.0 159.4 jit_solution(13172185858057545371)
XLA Ops:
  0.7 0.8 fusion.11
  1.8 1.3 dynamic-slice_bitcast_fusion
  3.1 1.4 collective-permute-start.1
  4.6 0.7 pad_maximum_fusion.1
  5.3 8.9 %collective-permute-start = (bf16[272,512]{1,0:T(8,128)(2,1)}, bf16[272,512]{1,0:T(8,128)(2,1)}, u32[]{:S(2)}, u32[]{:S(2)}) collective-permute-start(bf16[272,512]{1,0:T(8,128)(2,1)} %pad_maximum_fusion.1), channel_id=1, source_target_pairs={{0,1},{1,2},{3,0},{4,5},{5,6},{7,4},{8,9},{9,10},{11,8},{12,13},{1... | collective-permute-start | bytes 835592 | tf_op jit(solution)/shard_map/ppermute | solution.py:583
  14.2 0.7 pad_maximum_fusion.3
  14.9 1.9 %collective-permute-start.2 = (bf16[272,512]{1,0:T(8,128)(2,1)}, bf16[272,512]{1,0:T(8,128)(2,1)}, u32[]{:S(2)}, u32[]{:S(2)}) collective-permute-start(bf16[272,512]{1,0:T(8,128)(2,1)} %pad_maximum_fusion.3), channel_id=1, source_target_pairs={{1,0},{2,1},{3,2},{5,4},{6,5},{7,6},{9,8},{10,9},{11,10},{13,12},{... | collective-permute-start | bytes 835592 | tf_op jit(solution)/shard_map/ppermute | solution.py:583
  17.3 0.7 pad_maximum_fusion.part0
  21.1 2.0 %stack.27.meta = s32[8]{0:T(128)} concatenate(s32[1]{0:T(128)} %bitcast, s32[1]{0:T(128)} %bitcast.2, s32[1]{0:T(128)} %bitcast.3, s32[1]{0:T(128)} %bitcast.4, s32[1]{0:T(128)} %bitcast.5, s32[1]{0:T(128)} %bitcast.6, s32[1]{0:T(128)} %bitcast.7, s32[1]{0:T(128)} %bitcast.8), dimensions={0} | concatenate | bytes 64 | tf_op jit(solution)/shard_map/stack | solution.py:603
  23.1 0.8 fusion.7.mix_ref
  23.9 0.7 collective-permute-done.2.part3
  24.6 23.7 %shard_map.199 = (bf16[1024,512]{1,0:T(8,128)(2,1)}, bf16[1024,512]{1,0:T(8,128)(2,1)}, bf16[1024,512]{1,0:T(8,128)(2,1)}, bf16[1024,512]{1,0:T(8,128)(2,1)}, bf...) custom-call(s32[8]{0:T(128)} %stack.27.meta, ...), custom_call_target="tpu_custom_call" | custom-call | flops 10000000000 | bytes 20000000 | tf_op jit(solution)/shard_map/pallas_call | solution.py:438
  48.4 15.0 %collective-permute-start.3 = (bf16[16,192,128]{2,1,0:T(8,128)(2,1)}, bf16[16,192,128]{2,1,0:T(8,128)(2,1)S(1)}, u32[]{:S(2)}, u32[]{:S(2)}) collective-permute-start(bf16[16,192,128]{2,1,0:T(8,128)(2,1)} %get-tuple-element.44), channel_id=1, source_target_pairs={{0,1},{1,0},{2,3},{3,2},{4,5},{5,4},{6,7},{7,6},{8,9},{9,8},{10,11... | collective-permute-start | bytes 2359304 | tf_op jit(solution)/shard_map/ppermute | solution.py:588
  63.3 3.7 %shard_map.200.one_far = bf16[3,1024,128]{2,1,0:T(8,128)(2,1)} custom-call(s32[8]{0:T(128)} %stack.27.meta, bf16[1024,512]{1,0:T(8,128)(2,1)} %get-tuple-element.54.q_ref, bf16[1024,512]{1,0:T(8,128)(2,1)} %get-tuple-element.55.k_ref, bf16[1024,512]{1,0:T(8,128)(2,1)} %get-tuple-element.56.v_ref, bf16[1024,512]{1,0:T(8,128)(2,1)} %get-tuple-element.57.do_ref, ...), custom_call_target="tpu_custom_call" | custom-call | flops 4000000000 | bytes 2000000 | tf_op jit(solution)/shard_map/pallas_call | solution.py:468
  67.2 1.0 copy-done.1
  68.2 9.9 %all-to-all-start = ((bf16[16,208,128]{2,1,0:T(8,128)(2,1)}), bf16[16,208,128]{2,1,0:T(8,128)(2,1)S(1)}, u32[]{:S(2)}, u32[]{:S(2)}) async-start(bf16[16,208,128]{2,1,0:T(8,128)(2,1)} %copy-done.1), calls=%async_computation | async-start | bytes 1703936 | tf_op jit(solution)/shard_map/all_to_all | solution.py:620
  78.2 10.8 %shard_map.202 = (bf16[16,192,128]{2,1,0:T(8,128)(2,1)}, bf16[16,192,128]{2,1,0:T(8,128)(2,1)}, bf16[16,128]{1,0:T(8,128)(2,1)}) custom-call(s32[8]{0:T(128)} %stack.27.meta, bf16[1024,512]{1,0:T(8,128)(2,1)} %get-tuple-element.54.q_ref, bf16[1024,512]{1,0:T(8,128)(2,1)} %get-tuple-element.55.k_ref, bf16[1024,512]{1,0:T(8,128)(2,1)} %get-tuple-element.56.v_ref, ...), custom_call_target="tpu_custom_call" | custom-call | flops 16000000000 | bytes 10000000 | tf_op jit(solution)/shard_map/pallas_call | solution.py:491
  89.0 1.5 all-to-all-done.upper_ref
  90.5 10.1 %collective-permute-start.4 = (bf16[16,192,128]{2,1,0:T(8,128)(2,1)}, bf16[16,192,128]{2,1,0:T(8,128)(2,1)S(1)}, u32[]{:S(2)}, u32[]{:S(2)}) collective-permute-start(bf16[16,192,128]{2,1,0:T(8,128)(2,1)} %get-tuple-element.67), channel_id=1, source_target_pairs={{0,1},{1,0},{2,3},{3,2},{4,5},{5,4},{6,7},{7,6},{8,9},{9,8},{10,11... | collective-permute-start | bytes 2359304 | tf_op jit(solution)/shard_map/ppermute | solution.py:588
  100.6 2.1 %collective-permute-done.4.got_ref = bf16[16,192,128]{2,1,0:T(8,128)(2,1)S(1)} collective-permute-done((bf16[16,192,128]{2,1,0:T(8,128)(2,1)}, bf16[16,192,128]{2,1,0:T(8,128)(2,1)S(1)}, u32[]{:S(2)}, u32[]{:S(2)}) %collective-permute-start.4) | collective-permute-done | bytes 786464 | tf_op jit(solution)/shard_map/ppermute | solution.py:588
  102.7 1.1 copy-done.3
  103.8 0.7 copy-done.7
  104.7 20.9 %all_to_all.15.lower_ref = bf16[16,208,128]{2,1,0:T(8,128)(2,1)S(1)} all-to-all(bf16[16,208,128]{2,1,0:T(8,128)(2,1)S(1)} %shard_map.203), channel_id=1, replica_groups=mesh['z'=8,'ylo'=2,'x'=4,'yhi'=2,'core'=2] {'ylo','x','yhi'}, dimensions={0} | all-to-all | bytes 1703936 | tf_op jit(solution)/shard_map/all_to_all | solution.py:627
  125.6 1.4 shard_map.204
  127.0 18.6 %all_to_all.16.got_ref = bf16[8,176,128]{2,1,0:T(8,128)(2,1)S(1)} all-to-all(bf16[8,176,128]{2,1,0:T(8,128)(2,1)S(1)} %shard_map.204), channel_id=1, replica_groups=mesh['z'=8,'ylo'=2,'x'=4,'yhi'=2,'core'=2] {'z'}, dimensions={0} | all-to-all | bytes 720896 | tf_op jit(solution)/shard_map/all_to_all | solution.py:628
  145.7 0.8 shard_map.205
  146.4 3.9 %collective-permute-start.8 = (f32[128,128]{1,0:T(8,128)S(1)}, f32[128,128]{1,0:T(8,128)S(1)}, u32[]{:S(2)}, u32[]{:S(2)}) collective-permute-start(f32[128,128]{1,0:T(8,128)S(1)} %get-tuple-element.73.share_ref), channel_id=1, source_target_pairs={{0,1},{1,0},{2,3},{3,2},{4,5},{5,4},{6,7},{7,6},{8,9},{9,8},{10,11... | collective-permute-start | bytes 196616 | tf_op jit(solution)/shard_map/ppermute | solution.py:588
  150.4 0.9 collective-permute-start.5
  151.2 2.1 %collective-permute-start.6 = (f32[12,128]{1,0:T(8,128)S(1)}, f32[12,128]{1,0:T(8,128)S(1)}, u32[]{:S(2)}, u32[]{:S(2)}) collective-permute-start(f32[12,128]{1,0:T(8,128)S(1)} %get-tuple-element.71), channel_id=1, source_target_pairs={{0,2},{1,3},{2,0},{3,1},{4,6},{5,7},{6,4},{7,5},{8,10},{9,11},{10,... | collective-permute-start | bytes 18440 | tf_op jit(solution)/shard_map/ppermute | solution.py:632
  153.3 1.9 %collective-permute-done.6.row2 = f32[12,128]{1,0:T(8,128)S(1)} collective-permute-done((f32[12,128]{1,0:T(8,128)S(1)}, f32[12,128]{1,0:T(8,128)S(1)}, u32[]{:S(2)}, u32[]{:S(2)}) %collective-permute-start.6) | collective-permute-done | bytes 6176 | tf_op jit(solution)/shard_map/ppermute | solution.py:632
  155.2 2.6 %collective-permute-done.7.row3 = f32[12,128]{1,0:T(8,128)S(1)} collective-permute-done((f32[12,128]{1,0:T(8,128)S(1)}, f32[12,128]{1,0:T(8,128)S(1)}, u32[]{:S(2)}, u32[]{:S(2)}) %collective-permute-start.7) | collective-permute-done | bytes 6176 | tf_op jit(solution)/shard_map/ppermute | solution.py:632
  157.9 1.3 shard_map.206
  (43 shorter events, 3.5 us)
Async XLA Ops:
  0.6 16.2 %copy-start = (bf16[1024,1024]{1,0:T(8,128)(2,1)S(1)}, bf16[1024,1024]{1,0:T(8,128)(2,1)}, u32[]{:S(2)}) copy-start(bf16[1024,1024]{1,0:T(8,128)(2,1)} %param.29) | copy-start | bytes 6291460
  1.6 15.3 %copy-start.9 = (bf16[3,1024]{1,0:T(4,128)(2,1)S(1)}, bf16[3,1024]{1,0:T(4,128)(2,1)}, u32[]{:S(2)}) copy-start(bf16[3,1024]{1,0:T(4,128)(2,1)} %param.19) | copy-start | bytes 18436
  3.1 15.5 %copy-start.12 = (s32[3]{0:T(128)S(1)}, s32[3]{0:T(128)}, u32[]{:S(2)}) copy-start(s32[3]{0:T(128)} %param.17) | copy-start | bytes 40
  3.1 16.8 %copy-start.10 = (f32[1024]{0:T(1024)S(1)}, f32[1024]{0:T(1024)}, u32[]{:S(2)}) copy-start(f32[1024]{0:T(1024)} %param.30) | copy-start | bytes 12292
  3.1 17.3 %copy-start.11 = (s32[3,2]{0,1:T(2,128)S(1)}, s32[3,2]{0,1:T(2,128)}, u32[]{:S(2)}) copy-start(s32[3,2]{0,1:T(2,128)} %param.20) | copy-start | bytes 76
  3.1 20.0 %copy-start.8 = (bf16[1024,512]{1,0:T(8,128)(2,1)S(1)}, bf16[1024,512]{1,0:T(8,128)(2,1)}, u32[]{:S(2)}) copy-start(bf16[1024,512]{1,0:T(8,128)(2,1)} %param.23) | copy-start | bytes 3145732
  3.1 20.8 %collective-permute-start.1 = (bf16[272,512]{1,0:T(8,128)(2,1)S(1)}, bf16[272,512]{1,0:T(8,128)(2,1)}, u32[]{:S(2)}, u32[]{:S(2)}) collective-permute-start(bf16[272,512]{1,0:T(8,128)(2,1)S(1)} %pad_maximum_fusion.2), channel_id=1, source_target_pairs={{0,2},{2,0},{3,1},{4,6},{6,4},{7,5},{8,10},{10,8},{11,9},{12,14},{... | collective-permute-start | bytes 835592 | tf_op jit(solution)/shard_map/ppermute | solution.py:583
  5.3 18.6 %collective-permute-start = (bf16[272,512]{1,0:T(8,128)(2,1)}, bf16[272,512]{1,0:T(8,128)(2,1)}, u32[]{:S(2)}, u32[]{:S(2)}) collective-permute-start(bf16[272,512]{1,0:T(8,128)(2,1)} %pad_maximum_fusion.1), channel_id=1, source_target_pairs={{0,1},{1,2},{3,0},{4,5},{5,6},{7,4},{8,9},{9,10},{11,8},{12,13},{1... | collective-permute-start | bytes 835592 | tf_op jit(solution)/shard_map/ppermute | solution.py:583
  14.9 9.7 %collective-permute-start.2 = (bf16[272,512]{1,0:T(8,128)(2,1)}, bf16[272,512]{1,0:T(8,128)(2,1)}, u32[]{:S(2)}, u32[]{:S(2)}) collective-permute-start(bf16[272,512]{1,0:T(8,128)(2,1)} %pad_maximum_fusion.3), channel_id=1, source_target_pairs={{1,0},{2,1},{3,2},{5,4},{6,5},{7,6},{9,8},{10,9},{11,10},{13,12},{... | collective-permute-start | bytes 835592 | tf_op jit(solution)/shard_map/ppermute | solution.py:583
  48.4 18.7 %collective-permute-start.3 = (bf16[16,192,128]{2,1,0:T(8,128)(2,1)}, bf16[16,192,128]{2,1,0:T(8,128)(2,1)S(1)}, u32[]{:S(2)}, u32[]{:S(2)}) collective-permute-start(bf16[16,192,128]{2,1,0:T(8,128)(2,1)} %get-tuple-element.44), channel_id=1, source_target_pairs={{0,1},{1,0},{2,3},{3,2},{4,5},{5,4},{6,7},{7,6},{8,9},{9,8},{10,11... | collective-permute-start | bytes 2359304 | tf_op jit(solution)/shard_map/ppermute | solution.py:588
  63.3 3.7 %copy-start.2 = (bf16[16,192,128]{2,1,0:T(8,128)(2,1)S(1)}, bf16[16,192,128]{2,1,0:T(8,128)(2,1)}, u32[]{:S(2)}) copy-start(bf16[16,192,128]{2,1,0:T(8,128)(2,1)} %get-tuple-element.43.own_ref) | copy-start | bytes 2359300
  63.3 3.7 %copy-start.6 = (bf16[16,128]{1,0:T(8,128)(2,1)S(1)}, bf16[16,128]{1,0:T(8,128)(2,1)}, u32[]{:S(2)}) copy-start(bf16[16,128]{1,0:T(8,128)(2,1)} %get-tuple-element.52.packet_ref) | copy-start | bytes 12292
  67.2 1.0 copy-start.1
  68.2 22.2 %all-to-all-start = ((bf16[16,208,128]{2,1,0:T(8,128)(2,1)}), bf16[16,208,128]{2,1,0:T(8,128)(2,1)S(1)}, u32[]{:S(2)}, u32[]{:S(2)}) async-start(bf16[16,208,128]{2,1,0:T(8,128)(2,1)} %copy-done.1), calls=%async_computation | async-start | bytes 1703936 | tf_op jit(solution)/shard_map/all_to_all | solution.py:620
  78.2 47.4 %copy-start.4 = (f32[1024,2]{0,1:T(2,128)S(1)}, f32[1024,2]{0,1:T(2,128)}, u32[]{:S(2)}) copy-start(f32[1024,2]{0,1:T(2,128)} %param.31) | copy-start | bytes 24580
  89.0 36.6 %copy-start.5 = (s32[8]{0:T(128)S(1)}, s32[8]{0:T(128)}, u32[]{:S(2)}) copy-start(s32[8]{0:T(128)} %stack.27.meta) | copy-start | bytes 100
  90.5 12.2 %collective-permute-start.4 = (bf16[16,192,128]{2,1,0:T(8,128)(2,1)}, bf16[16,192,128]{2,1,0:T(8,128)(2,1)S(1)}, u32[]{:S(2)}, u32[]{:S(2)}) collective-permute-start(bf16[16,192,128]{2,1,0:T(8,128)(2,1)} %get-tuple-element.67), channel_id=1, source_target_pairs={{0,1},{1,0},{2,3},{3,2},{4,5},{5,4},{6,7},{7,6},{8,9},{9,8},{10,11... | collective-permute-start | bytes 2359304 | tf_op jit(solution)/shard_map/ppermute | solution.py:588
  102.7 1.1 copy-start.3
  103.8 0.7 copy-start.7
  146.4 11.5 %collective-permute-start.8 = (f32[128,128]{1,0:T(8,128)S(1)}, f32[128,128]{1,0:T(8,128)S(1)}, u32[]{:S(2)}, u32[]{:S(2)}) collective-permute-start(f32[128,128]{1,0:T(8,128)S(1)} %get-tuple-element.73.share_ref), channel_id=1, source_target_pairs={{0,1},{1,0},{2,3},{3,2},{4,5},{5,4},{6,7},{7,6},{8,9},{9,8},{10,11... | collective-permute-start | bytes 196616 | tf_op jit(solution)/shard_map/ppermute | solution.py:588
  150.4 3.0 %collective-permute-start.5 = (f32[12,128]{1,0:T(8,128)S(1)}, f32[12,128]{1,0:T(8,128)S(1)}, u32[]{:S(2)}, u32[]{:S(2)}) collective-permute-start(f32[12,128]{1,0:T(8,128)S(1)} %get-tuple-element.70), channel_id=1, source_target_pairs={{0,1},{1,2},{2,3},{3,0},{4,5},{5,6},{6,7},{7,4},{8,9},{9,10},{10,1... | collective-permute-start | bytes 18440 | tf_op jit(solution)/shard_map/ppermute | solution.py:632
  151.2 4.0 %collective-permute-start.6 = (f32[12,128]{1,0:T(8,128)S(1)}, f32[12,128]{1,0:T(8,128)S(1)}, u32[]{:S(2)}, u32[]{:S(2)}) collective-permute-start(f32[12,128]{1,0:T(8,128)S(1)} %get-tuple-element.71), channel_id=1, source_target_pairs={{0,2},{1,3},{2,0},{3,1},{4,6},{5,7},{6,4},{7,5},{8,10},{9,11},{10,... | collective-permute-start | bytes 18440 | tf_op jit(solution)/shard_map/ppermute | solution.py:632
  153.3 4.6 %collective-permute-start.7 = (f32[12,128]{1,0:T(8,128)S(1)}, f32[12,128]{1,0:T(8,128)S(1)}, u32[]{:S(2)}, u32[]{:S(2)}) collective-permute-start(f32[12,128]{1,0:T(8,128)S(1)} %get-tuple-element.72), channel_id=1, source_target_pairs={{0,3},{1,0},{2,1},{3,2},{4,7},{5,4},{6,5},{7,6},{8,11},{9,8},{10,9... | collective-permute-start | bytes 18440 | tf_op jit(solution)/shard_map/ppermute | solution.py:632
where the time goes:
time: 160 us; the launch traced here: 159 us
  starting transfers between devices  54.1 us (34%)
  Pallas kernels  42 us (26%)
  blocking collectives  39.5 us (25%)
  waiting for transfers between devices  8.87 us (6%)
  local copies, waits for them, and re-layouts  7.57 us (5%)
  other arithmetic  4.25 us (3%)
  between operations  1.9 us (1%)
    ppermute x3, starting transfers between devices, swap_cores(): return lax.ppermute(value, 'core', [(0, 1), (1, 0)])  29 us
    pallas_call x1, Pallas kernels, forward(): pl.pallas_call(forward_kernel, grid_spec=pltpu.PrefetchScalarGridSpec(num...  23.7 us
    all_to_all x1, blocking collectives, per_device(): lower_plane = lax.all_to_all(pieces, PLANE, 0, 0)  20.9 us
    all_to_all x1, blocking collectives, per_device(): lax.all_to_all(sum_pieces(meta, upper_plane, lower_plane, heads), 'z', 0, 0)  18.6 us
    ppermute x3, starting transfers between devices, to_samples(): got.append(lax.ppermute(part((me + k) % 4), CTX, pairs))  12.2 us
    pallas_call x1, Pallas kernels, rest_back(): pl.pallas_call(rest_kernel, grid_spec=pltpu.PrefetchScalarGridSpec(num_sc...  10.8 us
    all_to_all x1, starting transfers between devices, per_device(): upper_plane = lax.all_to_all(pieces, PLANE, 0, 0)  9.92 us
    ppermute x3, waiting for transfers between devices, per_device(): lax.ppermute(rows[k], CTX, [(i, (i + k) % 4) for i in range(4)])  4.58 us
  transfers between devices with their start and end apart: 10, of which 5 were waited for; matrix products, arithmetic and copies ran while one was open for 5% of the time, Pallas kernels for 9%

commit v1 on v0

--- a/solution.py
+++ b/solution.py
@@ -49,18 +49,18 @@
     return key <= query
 
 
-def spread(core, block_of, own_ref, other_ref):
+def spread(core, acc_ref, own_ref, other_ref):
     for mine in (0, 1):
 
         @pl.when(core == mine)
         def _():
-            for quarter in range(4):
-                target = own_ref if quarter // 2 == mine else other_ref
-                lanes = slice(quarter * 128, (quarter + 1) * 128)
-                for n in range(4):
-                    for a in range(8):
-                        start = n * 384 + a * 48
-                        target[2 * a + quarter % 2, n * 48 : (n + 1) * 48, :] = block_of(start, lanes)
+            for block in range(acc_ref.shape[1] // 128):
+                target = own_ref if block % 2 == mine else other_ref
+                lanes = slice(block * 128, (block + 1) * 128)
+                place = slice(block // 2 * 96, (block // 2 + 1) * 96)
+                for g in range(16):
+                    rows = [acc_ref[n * 384 + g * 24 : n * 384 + (g + 1) * 24, lanes] for n in range(4)]
+                    target[g, place, :] = jnp.concatenate(rows, axis=0).astype(BF16)
 
 
 def forward_kernel(
@@ -226,9 +226,7 @@
 
     @pl.when(step == 2 * BLOCKS - 1)
     def _():
-        spread(
-            meta[6], lambda row, lanes: term_acc[row : row + 48, lanes].astype(BF16), own_ref, other_ref
-        )
+        spread(meta[6], term_acc, own_ref, other_ref)
 
 
 def pair_body(
@@ -271,24 +269,17 @@
     dv_ref[...] = dv_acc[...].astype(BF16)
 
 
-def pair_kernel(
-    meta, q_ref, k_ref, v_ref, do_ref, lse_ref, delta_ref, grad_ref, dk_acc, dv_acc, kt_ref
-):
-    pair_body(
-        meta[1], q_ref, k_ref, v_ref, do_ref, lse_ref, delta_ref,
-        grad_ref.at[0], grad_ref.at[1], grad_ref.at[2], dk_acc, dv_acc, kt_ref,
-    )
-
-
-def rest_kernel(
-    meta, q_ref, k_ref, v_ref, do_ref, lse_ref, delta_ref, logit_ref,
-    one_far, mixed_far, normed_far, wq_far, wk_far, wv_far,
-    own_ref, other_ref, packet_ref,
-    dk_acc, dv_acc, kt_ref, term_ref, grad_ref, one_ref, mixed_ref, normed_ref, wq_ref, wk_ref, wv_ref, sems,
+def pairs_kernel(
+    first,
+    meta, q_ref, k_ref, v_ref, do_ref, lse_ref, delta_ref, logit_ref, prior_ref,
+    mixed_far, normed_far, wq_far, wk_far, wv_far,
+    own_ref, other_ref, sums_ref, packet_ref,
+    dk_acc, dv_acc, kt_ref, term_ref, grad_ref, mixed_ref, normed_ref, wq_ref, wk_ref, wv_ref, sems,
 ):
     step = pl.program_id(0)
-    far = (one_far, mixed_far, normed_far, wq_far, wk_far, wv_far)
-    near = (one_ref, mixed_ref, normed_ref, wq_ref, wk_ref, wv_ref)
+    columns = pl.ds(first * 128, 256)
+    far = (mixed_far, normed_far) + tuple(w.at[:, columns] for w in (wq_far, wk_far, wv_far))
+    near = (mixed_ref, normed_ref, wq_ref, wk_ref, wv_ref)
     copies = [pltpu.make_async_copy(f, n, sems.at[i]) for i, (f, n) in enumerate(zip(far, near))]
 
     @pl.when(step == 0)
@@ -301,20 +292,21 @@
         grad_ref.at[0, step], grad_ref.at[1, step], grad_ref.at[2, step], dk_acc, dv_acc, kt_ref,
     )
 
-    @pl.when(step == 2)
+    @pl.when(step == 1)
     def _():
         for copy in copies:
             copy.wait()
         turned = mixed_ref[...].T
         total = None
         for n, weight in enumerate((wq_ref, wk_ref, wv_ref)):
-            rows = jnp.concatenate([one_ref[n]] + [grad_ref[n, p] for p in range(3)], axis=1)
-            term_ref[n * D : (n + 1) * D, :] = dot(turned, rows).astype(BF16)
+            rows = jnp.concatenate([grad_ref[n, 0], grad_ref[n, 1]], axis=1)
+            term_ref[n * D : (n + 1) * D, :] = dot(turned, rows)
             part = dot_nt(rows, weight[...])
             total = part if total is None else total + part
-        spread(meta[6], lambda row, lanes: term_ref[row : row + 48, lanes], own_ref, other_ref)
-        mix = jnp.sum(total, axis=0, keepdims=True)
-        gain = jnp.sum(total * normed_ref[...].astype(F32), axis=0, keepdims=True)
+        spread(meta[6], term_ref, own_ref, other_ref)
+        mix = jnp.sum(total, axis=0, keepdims=True) + prior_ref[0:1, :]
+        gain = jnp.sum(total * normed_ref[...].astype(F32), axis=0, keepdims=True) + prior_ref[1:2, :]
+        sums_ref[...] = jnp.concatenate([mix, gain], axis=0)
         logit = logit_ref[...]
         high = logit.astype(BF16).astype(F32)
         lines = [mix[:, n * 128 : (n + 1) * 128] for n in range(4)]
@@ -323,11 +315,16 @@
         packet_ref[...] = jnp.concatenate(lines, axis=0).astype(BF16)
 
 
-def piece_kernel(own_ref, got_ref, packet_ref, piece_ref):
+def piece_kernel(packet_ref, *refs):
+    *halves, piece_ref = refs
     for g in range(16):
-        total = own_ref[g].astype(F32) + got_ref[g].astype(F32)
-        piece_ref[g, :192, :] = total.astype(BF16)
-        piece_ref[g, 192:, :] = packet_ref[...]
+        start = 0
+        for own_ref, got_ref in zip(halves[::2], halves[1::2]):
+            count = own_ref.shape[1]
+            total = own_ref[g].astype(F32) + got_ref[g].astype(F32)
+            piece_ref[g, start : start + count, :] = total.astype(BF16)
+            start += count
+        piece_ref[g, start:, :] = packet_ref[...]
 
 
 def exact_dot(a, b):
@@ -338,17 +335,20 @@
 
 
 def sum_kernel(meta, upper_ref, lower_ref, heads_ref, piece_ref):
-    upper_packets = [upper_ref[g, 192:, :].astype(F32) for g in range(16)]
-    lower_packets = [lower_ref[g, 192:, :].astype(F32) for g in range(16)]
+    upper_packets = [upper_ref[g, 288:, :].astype(F32) for g in range(16)]
+    lower_packets = [lower_ref[g, 96:, :].astype(F32) for g in range(16)]
 
     def pick(packets, row):
         return jnp.concatenate([p[row : row + 1, :] for p in packets], axis=0)
 
-    upper = functools.reduce(jnp.add, [upper_ref[g, :192, :].astype(F32) for g in range(16)])
-    lower = functools.reduce(jnp.add, [lower_ref[g, :192, :].astype(F32) for g in range(16)])
+    first = functools.reduce(jnp.add, [upper_ref[g, :288, :].astype(F32) for g in range(16)])
+    second = functools.reduce(jnp.add, [lower_ref[g, :96, :].astype(F32) for g in range(16)])
     for n in range(4):
-        piece_ref[n, :48, :] = lower[n * 48 : (n + 1) * 48].astype(BF16)
-        piece_ref[4 + n, :48, :] = upper[n * 48 : (n + 1) * 48].astype(BF16)
+        here = slice(n * 24, (n + 1) * 24)
+        rows = jnp.concatenate([first[192:][here], second[here]], axis=0)
+        piece_ref[n, :48, :] = rows.astype(BF16)
+        rows = jnp.concatenate([first[:96][here], first[96:192][here]], axis=0)
+        piece_ref[4 + n, :48, :] = rows.astype(BF16)
     logits = pick(lower_packets, 8) + pick(lower_packets, 9)
     grad_a, grad_c = logits[:, 0:1], logits[:, 1:2]
     lane = lax.broadcasted_iota(jnp.int32, (8, 128), 1)
@@ -375,42 +375,44 @@
         piece_ref[z, 144:176, :] = flat
 
 
-def final_kernel(meta, got_ref, row0, row1, row2, row3, share_ref):
+def final_kernel(meta, got_ref, kept_ref, sent_ref):
     total = functools.reduce(jnp.add, [got_ref[z].astype(F32) for z in range(8)])
-    for n in range(4):
-        for k, ref in enumerate((row0, row1, row2, row3)):
-
-            @pl.when(lax.rem(meta[0] + k, 4) == n)
-            def _():
-                ref[...] = total[n * 12 : (n + 1) * 12, :]
-
-    share_ref[...] = total[48:176, :]
-
-
-def join_kernel(meta, row0, row1, row2, row3, share_ref, swapped_ref, sequence_ref, mix_ref, cross_ref, gain_ref, bias_ref, heads_ref):
-    for source, place in ((0, 0), (2, 1), (1, 2), (3, 3)):
-        entry = lax.rem(meta[0] - source + 4, 4)
-        for n, ref in enumerate((row0, row1, row2, row3)):
-
-            @pl.when(entry == n)
-            def _():
-                sequence_ref[:, place * 128 : (place + 1) * 128] = ref[...]
-
-    total = share_ref[...] + swapped_ref[...]
-    upper = meta[6] == 1
-    for r in range(12):
-        mine = jnp.where(upper, total[r * 8 + 4 : r * 8 + 8, :], total[r * 8 : r * 8 + 4, :])
-        if r < 8:
-            cross_ref[:, r * 128 : (r + 1) * 128] = mine
-        else:
-            mix_ref[:, (r - 8) * 128 : (r - 7) * 128] = mine
+
+    def of_core(core):
+        rows = [total[n * 24 + core * 12 : n * 24 + (core + 1) * 12, :] for n in range(2)]
+        rows += [total[48 + r * 8 + core * 4 : 52 + r * 8 + core * 4, :] for r in range(12)]
+        return jnp.concatenate(rows + [total[144:176, :]], axis=0)
+
+    for core in (0, 1):
+
+        @pl.when(meta[6] == core)
+        def _():
+            kept_ref[...] = of_core(core)
+            sent_ref[...] = of_core(1 - core)
+
+
+def join_kernel(meta, kept_ref, got_ref, sequence_ref, mix_ref, cross_ref, gain_ref, bias_ref, heads_ref):
+    for core in (0, 1):
+
+        @pl.when(meta[6] == core)
+        def _():
+            for n in range(2):
+                for ref, owner in ((kept_ref, core), (got_ref, 1 - core)):
+                    start = n * 256 + owner * 128
+                    sequence_ref[:, start : start + 128] = ref[n * 12 : (n + 1) * 12, :]
+
+    total = kept_ref[...] + got_ref[...]
+    for r in range(8):
+        cross_ref[:, r * 128 : (r + 1) * 128] = total[24 + r * 4 : 28 + r * 4, :]
     for r in range(4):
-        gain_ref[:, r * 128 : (r + 1) * 128] = total[96 + r : 97 + r, :]
+        lanes = slice(r * 128, (r + 1) * 128)
+        mix_ref[:, lanes] = total[56 + r * 4 : 60 + r * 4, :]
+        gain_ref[:, lanes] = total[72 + r : 73 + r, :]
     for r in range(8):
         lanes = slice(r * 128, (r + 1) * 128)
-        bias_ref[:, lanes] = total[100 + r : 101 + r, :]
-        heads_ref[0:1, lanes] = total[108 + r : 109 + r, :]
-        heads_ref[1:2, lanes] = total[116 + r : 117 + r, :]
+        bias_ref[:, lanes] = total[76 + r : 77 + r, :]
+        heads_ref[0:1, lanes] = total[84 + r : 85 + r, :]
+        heads_ref[1:2, lanes] = total[92 + r : 93 + r, :]
 
 
 def whole(shape):
@@ -462,61 +464,42 @@
     )(meta, *small, *large)
 
 
-def first_pair_back(meta, queries, keys, values, grads, lse, delta):
-    lanes = pl.BlockSpec((LEN, 128), lambda i, m: (0, i))
-    pair = pl.BlockSpec((1, 2, LEN), lambda i, m: (i, 0, 0))
+def pairs_back(meta, first, queries, keys, values, grads, lse, delta, logit, prior, *far):
+    lanes = pl.BlockSpec((LEN, 128), lambda i, m: (0, first + i))
+    pair = pl.BlockSpec((1, 2, LEN), lambda i, m: (first + i, 0, 0))
+    outs = [((16, 96, 128), BF16), ((16, 96, 128), BF16), ((2, D), F32), ((16, 128), BF16)]
     return pl.pallas_call(
-        pair_kernel,
+        functools.partial(pairs_kernel, first),
         grid_spec=pltpu.PrefetchScalarGridSpec(
             num_scalar_prefetch=1,
-            grid=(1,),
-            in_specs=[lanes] * 4 + [pair] * 2,
-            out_specs=whole((3, LEN, 128)),
+            grid=(2,),
+            in_specs=[lanes] * 4 + [pair] * 2 + [whole(logit.shape), whole(prior.shape)]
+            + [pl.BlockSpec(memory_space=pl.ANY)] * 5,
+            out_specs=[whole(s) for s, _ in outs],
             scratch_shapes=[
                 pltpu.VMEM((LEN, 128), F32),
                 pltpu.VMEM((LEN, 128), F32),
                 pltpu.VMEM((128, LEN), BF16),
-            ],
+                pltpu.VMEM((3 * D, 256), F32),
+                pltpu.VMEM((3, 2, LEN, 128), BF16),
+                pltpu.VMEM((LEN, D), BF16),
+                pltpu.VMEM((LEN, D), BF16),
+            ] + [pltpu.VMEM((D, 256), BF16)] * 3 + [pltpu.SemaphoreType.DMA((5,))],
         ),
-        out_shape=jax.ShapeDtypeStruct((3, LEN, 128), BF16),
+        out_shape=[jax.ShapeDtypeStruct(s, t) for s, t in outs],
         compiler_params=params(60),
-        cost_estimate=cost(4 * 10**9, 2 * 10**6, 2 * 10**6),
-    )(meta, queries, keys, values, grads, lse, delta)
-
-
-def rest_back(meta, queries, keys, values, grads, lse, delta, logit, *far):
-    lanes = pl.BlockSpec((LEN, 128), lambda i, m: (0, 1 + i))
-    pair = pl.BlockSpec((1, 2, LEN), lambda i, m: (1 + i, 0, 0))
-    outs = ((16, 192, 128), (16, 192, 128), (16, 128))
-    return pl.pallas_call(
-        rest_kernel,
-        grid_spec=pltpu.PrefetchScalarGridSpec(
-            num_scalar_prefetch=1,
-            grid=(3,),
-            in_specs=[lanes] * 4 + [pair] * 2 + [whole(logit.shape)]
-            + [pl.BlockSpec(memory_space=pl.ANY)] * 6,
-            out_specs=[whole(s) for s in outs],
-            scratch_shapes=[
-                pltpu.VMEM((LEN, 128), F32),
-                pltpu.VMEM((LEN, 128), F32),
-                pltpu.VMEM((128, LEN), BF16),
-                pltpu.VMEM((3 * D, D), BF16),
-                pltpu.VMEM((3, 3, LEN, 128), BF16),
-            ] + [pltpu.VMEM(a.shape, BF16) for a in far] + [pltpu.SemaphoreType.DMA((6,))],
-        ),
-        out_shape=[jax.ShapeDtypeStruct(s, BF16) for s in outs],
-        compiler_params=params(60),
-        cost_estimate=cost(16 * 10**9, 10**7, 6 * 10**6),
-    )(meta, queries, keys, values, grads, lse, delta, logit, *far)
-
-
-def cut_pieces(own, got, packet):
+        cost_estimate=cost(10**10, 10**7, 4 * 10**6),
+    )(meta, queries, keys, values, grads, lse, delta, logit, prior, *far)
+
+
+def cut_pieces(packet, *halves):
+    count = sum(h.shape[1] for h in halves[::2]) + packet.shape[0]
     return pl.pallas_call(
         piece_kernel,
-        out_shape=jax.ShapeDtypeStruct((16, 208, 128), BF16),
+        out_shape=jax.ShapeDtypeStruct((16, count, 128), BF16),
         compiler_params=pltpu.CompilerParams(vmem_limit_bytes=16 * 2**20),
         cost_estimate=cost(10**6, 3 * 10**6),
-    )(own, got, packet)
+    )(packet, *halves)
 
 
 def sum_pieces(meta, upper, lower, heads):
@@ -535,7 +518,7 @@
 
 
 def total_rows(meta, got):
-    outs = ((12, 128),) * 4 + ((128, 128),)
+    outs = ((104, 128),) * 2
     return pl.pallas_call(
         final_kernel,
         grid_spec=pltpu.PrefetchScalarGridSpec(
@@ -550,9 +533,8 @@
     )(meta, got)
 
 
-def join(meta, rows, share, swapped):
+def join(meta, *args):
     outs = ((12, D), (4, D), (4, DI), (1, D), (1, DI), (2, DI))
-    args = (*rows, share, swapped)
     return pl.pallas_call(
         join_kernel,
         grid_spec=pltpu.PrefetchScalarGridSpec(
@@ -611,27 +593,22 @@
         (*parts, mix_row, seq_gain[None], base, dense.astype(F32), heads),
         (event_table, w_query, w_key, w_value, w_out, w_pool),
     )
-    upper_got = swap_cores(other)
-    attention = (queries, keys, values, grads, lse, delta)
-    one = first_pair_back(meta, *attention)
-    upper_got, one = lax.optimization_barrier((upper_got, one))
-    pieces = cut_pieces(own, upper_got, packet)
+    got = swap_cores(other)
+    attention = (queries, keys, values, grads, lse, delta, logit)
+    rest = (mixed, normed, w_query, w_key, w_value)
+    own_first, other_first, sums, _ = pairs_back(
+        meta, 0, *attention, jnp.zeros((2, D), F32), *rest
+    )
+    got, other_first = lax.optimization_barrier((got, other_first))
+    pieces = cut_pieces(packet, own, got, own_first, swap_cores(other_first))
     pieces, attention = lax.optimization_barrier((pieces, attention))
     upper_plane = lax.all_to_all(pieces, PLANE, 0, 0)
-    own, other, packet = rest_back(
-        meta, *attention, logit, one, mixed, normed, w_query, w_key, w_value
-    )
-    upper_plane, other = lax.optimization_barrier((upper_plane, other))
-    lower_got = swap_cores(other)
-    pieces = cut_pieces(own, lower_got, packet)
+    own, other, _, packet = pairs_back(meta, 2, *attention, sums, *rest)
+    pieces = cut_pieces(packet, own, swap_cores(other))
     lower_plane = lax.all_to_all(pieces, PLANE, 0, 0)
     got = lax.all_to_all(sum_pieces(meta, upper_plane, lower_plane, heads), "z", 0, 0)
-    *rows, share = total_rows(meta, got)
-    entries = rows[:1]
-    for k in (1, 2, 3):
-        entries.append(lax.ppermute(rows[k], CTX, [(i, (i + k) % 4) for i in range(4)]))
-    swapped = swap_cores(share)
-    sequence, mix, cross, gain, bias, grad_heads = join(meta, entries, share, swapped)
+    kept, sent = total_rows(meta, got)
+    sequence, mix, cross, gain, bias, grad_heads = join(meta, kept, swap_cores(sent))
     return (sequence, mix, cross, gain.reshape(D), bias.reshape(DI), grad_heads.T)
 
 

time: 160 us -> 161 us (level)
  blocking collectives: 39.5 us -> 57.5 us
  Pallas kernels: 42 us -> 33.1 us
  starting transfers between devices: 54.1 us -> 45.9 us
  waiting for transfers between devices: 8.87 us -> 4.72 us
  local copies, waits for them, and re-layouts: 7.57 us -> 11.1 us
    all_to_all x0 -> x1, blocking collectives: none -> 21.3 us  [per_device(): upper_plane = lax.all_to_all(pieces, PLANE, 0, 0)]
    all_to_all x1 -> x0, starting transfers between devices: 9.92 us -> none  [per_device(): upper_plane = lax.all_to_all(pieces, PLANE, 0, 0)]
    pallas_call x1, Pallas kernels: 23.7 us -> 15.1 us  [forward(): pl.pallas_call(forward_kernel, grid_spec=pltpu.PrefetchScalarGridSpec(num...]
    all_to_all x1, blocking collectives: 20.9 us -> 14.3 us  [per_device(): lower_plane = lax.all_to_all(pieces, PLANE, 0, 0)]
    ppermute x3 -> x4, starting transfers between devices: 29 us -> 33.7 us  [swap_cores(): return lax.ppermute(value, 'core', [(0, 1), (1, 0)])]
    ppermute x3 -> x0, waiting for transfers between devices: 4.58 us -> none  [per_device(): lax.ppermute(rows[k], CTX, [(i, (i + k) % 4) for i in range(4)])]
    all_to_all x1, blocking collectives: 18.6 us -> 21.9 us  [per_device(): lax.all_to_all(sum_pieces(meta, upper_plane, lower_plane, heads), 'z', 0, 0)]
    unnamed x30 -> x34, local copies, waits for them, and re-layouts: 2.91 us -> 5.91 us
  transfers between devices with their start and end apart: 10 -> 7, of which waited for: 5 -> 4; matrix products, arithmetic and copies ran while one was open for 5% -> 5% of each run, Pallas kernels for 9% -> 4%
where the time goes in v1:
time: 161 us; the launch traced here: 160 us
  blocking collectives  57.5 us (36%)
  starting transfers between devices  45.9 us (29%)
  Pallas kernels  33.1 us (21%)
  local copies, waits for them, and re-layouts  11.1 us (7%)
  waiting for transfers between devices  4.72 us (3%)
  other arithmetic  4.29 us (3%)
  between operations  1.88 us (1%)
    ppermute x4, starting transfers between devices, swap_cores(): return lax.ppermute(value, 'core', [(0, 1), (1, 0)])  33.7 us
    all_to_all x1, blocking collectives, per_device(): lax.all_to_all(sum_pieces(meta, upper_plane, lower_plane, heads), 'z', 0, 0)  21.9 us
    all_to_all x1, blocking collectives, per_device(): upper_plane = lax.all_to_all(pieces, PLANE, 0, 0)  21.3 us
    pallas_call x1, Pallas kernels, forward(): pl.pallas_call(forward_kernel, grid_spec=pltpu.PrefetchScalarGridSpec(num...  15.1 us
    pallas_call x2, Pallas kernels, pairs_back(): pl.pallas_call(functools.partial(pairs_kernel, first), grid_spec=pltpu.Pr...  14.4 us
    all_to_all x1, blocking collectives, per_device(): lower_plane = lax.all_to_all(pieces, PLANE, 0, 0)  14.3 us
    ppermute x3, starting transfers between devices, to_samples(): got.append(lax.ppermute(part((me + k) % 4), CTX, pairs))  12.2 us
    unnamed x34, local copies, waits for them, and re-layouts  5.91 us
  transfers between devices with their start and end apart: 7, of which 4 were waited for; matrix products, arithmetic and copies ran while one was open for 5% of the time, Pallas kernels for 4%

profile of v1, /device:TPU:1, one launch (start us, length us, event | category | flops | bytes accessed | tf_op | source)
XLA Modules:
  0.0 159.8 jit_solution(18025683169847472085)
XLA Ops:
  0.7 0.8 fusion.11
  1.8 1.3 dynamic-slice_bitcast_fusion
  3.2 1.4 collective-permute-start.1
  4.6 0.7 pad_maximum_fusion.1
  5.3 8.9 %collective-permute-start = (bf16[272,512]{1,0:T(8,128)(2,1)}, bf16[272,512]{1,0:T(8,128)(2,1)}, u32[]{:S(2)}, u32[]{:S(2)}) collective-permute-start(bf16[272,512]{1,0:T(8,128)(2,1)} %pad_maximum_fusion.1), channel_id=1, source_target_pairs={{0,1},{1,2},{3,0},{4,5},{5,6},{7,4},{8,9},{9,10},{11,8},{12,13},{1... | collective-permute-start | bytes 835592 | tf_op jit(solution)/shard_map/ppermute | solution.py:565
  14.2 0.7 pad_maximum_fusion.3
  15.0 1.9 %collective-permute-start.2 = (bf16[272,512]{1,0:T(8,128)(2,1)}, bf16[272,512]{1,0:T(8,128)(2,1)}, u32[]{:S(2)}, u32[]{:S(2)}) collective-permute-start(bf16[272,512]{1,0:T(8,128)(2,1)} %pad_maximum_fusion.3), channel_id=1, source_target_pairs={{1,0},{2,1},{3,2},{5,4},{6,5},{7,6},{9,8},{10,9},{11,10},{13,12},{... | collective-permute-start | bytes 835592 | tf_op jit(solution)/shard_map/ppermute | solution.py:565
  17.3 0.8 pad_maximum_fusion.part0
  21.2 1.9 %stack.27.meta = s32[8]{0:T(128)} concatenate(s32[1]{0:T(128)} %bitcast, s32[1]{0:T(128)} %bitcast.2, s32[1]{0:T(128)} %bitcast.3, s32[1]{0:T(128)} %bitcast.4, s32[1]{0:T(128)} %bitcast.5, s32[1]{0:T(128)} %bitcast.6, s32[1]{0:T(128)} %bitcast.7, s32[1]{0:T(128)} %bitcast.8), dimensions={0} | concatenate | bytes 64 | tf_op jit(solution)/shard_map/stack | solution.py:585
  23.1 0.8 fusion.7.mix_ref
  23.9 0.7 collective-permute-done.2.part3
  24.6 15.1 %shard_map.199 = (bf16[1024,512]{1,0:T(8,128)(2,1)}, bf16[1024,512]{1,0:T(8,128)(2,1)}, bf16[1024,512]{1,0:T(8,128)(2,1)}, bf16[1024,512]{1,0:T(8,128)(2,1)}, bf...) custom-call(s32[8]{0:T(128)} %stack.27.meta, ...), custom_call_target="tpu_custom_call" | custom-call | flops 10000000000 | bytes 20000000 | tf_op jit(solution)/shard_map/pallas_call | solution.py:440
  39.8 15.0 %collective-permute-start.3 = (bf16[16,192,128]{2,1,0:T(8,128)(2,1)}, bf16[16,192,128]{2,1,0:T(8,128)(2,1)S(1)}, u32[]{:S(2)}, u32[]{:S(2)}) collective-permute-start(bf16[16,192,128]{2,1,0:T(8,128)(2,1)} %get-tuple-element.44), channel_id=1, source_target_pairs={{0,1},{1,0},{2,3},{3,2},{4,5},{5,4},{6,7},{7,6},{8,9},{9,8},{10,11... | collective-permute-start | bytes 2359304 | tf_op jit(solution)/shard_map/ppermute | solution.py:570
  55.4 7.2 %shard_map.200 = (bf16[16,96,128]{2,1,0:T(8,128)(2,1)}, bf16[16,96,128]{2,1,0:T(8,128)(2,1)}, f32[2,512]{1,0:T(2,128)}, bf16[16,128]{1,0:T(8,128)(2,1)}) custom-call(s32[8]{0:T(128)} %stack.27.meta, bf16[1024,512]{1,0:T(8,128)(2,1)} %get-tuple-element.59.q_ref, bf16[1024,512]{1,0:T(8,128)(2,1)} %get-tuple-element.60.k_ref, ...), custom_call_target="tpu_custom_call" | custom-call | flops 10000000000 | bytes 10000000 | tf_op jit(solution)/shard_map/pallas_call | solution.py:471
  62.6 0.9 copy-done.2
  63.5 6.9 %collective-permute-start.4 = (bf16[16,96,128]{2,1,0:T(8,128)(2,1)}, bf16[16,96,128]{2,1,0:T(8,128)(2,1)S(1)}, u32[]{:S(2)}, u32[]{:S(2)}) collective-permute-start(bf16[16,96,128]{2,1,0:T(8,128)(2,1)} %get-tuple-element.57), channel_id=1, source_target_pairs={{0,1},{1,0},{2,3},{3,2},{4,5},{5,4},{6,7},{7,6},{8,9},{9,8},{10,11... | collective-permute-start | bytes 1179656 | tf_op jit(solution)/shard_map/ppermute | solution.py:570
  70.4 1.6 collective-permute-done.4.refs_3_
  71.9 1.1 copy-done.1
  73.1 1.1 copy-done.3
  74.2 1.0 copy-done.5
  75.5 7.2 %shard_map.202 = (bf16[16,96,128]{2,1,0:T(8,128)(2,1)}, bf16[16,96,128]{2,1,0:T(8,128)(2,1)}, f32[2,512]{1,0:T(2,128)}, bf16[16,128]{1,0:T(8,128)(2,1)}) custom-call(s32[8]{0:T(128)} %stack.27.meta, bf16[1024,512]{1,0:T(8,128)(2,1)} %get-tuple-element.59.q_ref, bf16[1024,512]{1,0:T(8,128)(2,1)} %get-tuple-element.60.k_ref, ...), custom_call_target="tpu_custom_call" | custom-call | flops 10000000000 | bytes 10000000 | tf_op jit(solution)/shard_map/pallas_call | solution.py:471
  82.7 7.3 %collective-permute-start.5 = (bf16[16,96,128]{2,1,0:T(8,128)(2,1)}, bf16[16,96,128]{2,1,0:T(8,128)(2,1)S(1)}, u32[]{:S(2)}, u32[]{:S(2)}) collective-permute-start(bf16[16,96,128]{2,1,0:T(8,128)(2,1)} %get-tuple-element.69), channel_id=1, source_target_pairs={{0,1},{1,0},{2,3},{3,2},{4,5},{5,4},{6,7},{7,6},{8,9},{9,8},{10,11... | collective-permute-start | bytes 1179656 | tf_op jit(solution)/shard_map/ppermute | solution.py:570
  90.1 1.6 collective-permute-done.5.refs_1_
  91.6 1.0 copy-done.4
  92.6 0.7 copy-done.8
  93.4 14.3 %all_to_all.15.lower_ref = bf16[16,112,128]{2,1,0:T(8,128)(2,1)S(1)} all-to-all(bf16[16,112,128]{2,1,0:T(8,128)(2,1)S(1)} %shard_map.203), channel_id=1, replica_groups=mesh['z'=8,'ylo'=2,'x'=4,'yhi'=2,'core'=2] {'ylo','x','yhi'}, dimensions={0} | all-to-all | bytes 917504 | tf_op jit(solution)/shard_map/all_to_all | solution.py:608
  107.7 21.3 %all_to_all.16.upper_ref = bf16[16,304,128]{2,1,0:T(8,128)(2,1)S(1)} all-to-all(bf16[16,304,128]{2,1,0:T(8,128)(2,1)S(1)} %shard_map.201), channel_id=1, replica_groups=mesh['z'=8,'ylo'=2,'x'=4,'yhi'=2,'core'=2] {'ylo','x','yhi'}, dimensions={0} | all-to-all | bytes 2490368 | tf_op jit(solution)/shard_map/all_to_all | solution.py:605
  129.1 1.4 shard_map.204
  130.5 21.9 %all_to_all.17.got_ref = bf16[8,176,128]{2,1,0:T(8,128)(2,1)S(1)} all-to-all(bf16[8,176,128]{2,1,0:T(8,128)(2,1)S(1)} %shard_map.204), channel_id=1, replica_groups=mesh['z'=8,'ylo'=2,'x'=4,'yhi'=2,'core'=2] {'z'}, dimensions={0} | all-to-all | bytes 720896 | tf_op jit(solution)/shard_map/all_to_all | solution.py:609
  153.0 4.4 %collective-permute-start.6 = (f32[104,128]{1,0:T(8,128)S(1)}, f32[104,128]{1,0:T(8,128)S(1)}, u32[]{:S(2)}, u32[]{:S(2)}) collective-permute-start(f32[104,128]{1,0:T(8,128)S(1)} %get-tuple-element.71), channel_id=1, source_target_pairs={{0,1},{1,0},{2,3},{3,2},{4,5},{5,4},{6,7},{7,6},{8,9},{9,8},{10,11... | collective-permute-start | bytes 159752 | tf_op jit(solution)/shard_map/ppermute | solution.py:570
  157.4 0.9 collective-permute-done.6.got_ref
  158.3 1.2 shard_map.206
  (43 shorter events, 4.7 us)
Async XLA Ops:
  0.6 16.3 %copy-start = (bf16[1024,1024]{1,0:T(8,128)(2,1)S(1)}, bf16[1024,1024]{1,0:T(8,128)(2,1)}, u32[]{:S(2)}) copy-start(bf16[1024,1024]{1,0:T(8,128)(2,1)} %param.29) | copy-start | bytes 6291460
  1.6 15.3 %copy-start.11 = (bf16[3,1024]{1,0:T(4,128)(2,1)S(1)}, bf16[3,1024]{1,0:T(4,128)(2,1)}, u32[]{:S(2)}) copy-start(bf16[3,1024]{1,0:T(4,128)(2,1)} %param.19) | copy-start | bytes 18436
  3.1 15.6 %copy-start.14 = (s32[3]{0:T(128)S(1)}, s32[3]{0:T(128)}, u32[]{:S(2)}) copy-start(s32[3]{0:T(128)} %param.17) | copy-start | bytes 40
  3.1 16.8 %copy-start.12 = (f32[1024]{0:T(1024)S(1)}, f32[1024]{0:T(1024)}, u32[]{:S(2)}) copy-start(f32[1024]{0:T(1024)} %param.30) | copy-start | bytes 12292
  3.1 17.4 %copy-start.13 = (s32[3,2]{0,1:T(2,128)S(1)}, s32[3,2]{0,1:T(2,128)}, u32[]{:S(2)}) copy-start(s32[3,2]{0,1:T(2,128)} %param.20) | copy-start | bytes 76
  3.1 20.0 %copy-start.10 = (bf16[1024,512]{1,0:T(8,128)(2,1)S(1)}, bf16[1024,512]{1,0:T(8,128)(2,1)}, u32[]{:S(2)}) copy-start(bf16[1024,512]{1,0:T(8,128)(2,1)} %param.23) | copy-start | bytes 3145732
  3.2 20.8 %collective-permute-start.1 = (bf16[272,512]{1,0:T(8,128)(2,1)S(1)}, bf16[272,512]{1,0:T(8,128)(2,1)}, u32[]{:S(2)}, u32[]{:S(2)}) collective-permute-start(bf16[272,512]{1,0:T(8,128)(2,1)S(1)} %pad_maximum_fusion.2), channel_id=1, source_target_pairs={{0,2},{2,0},{3,1},{4,6},{6,4},{7,5},{8,10},{10,8},{11,9},{12,14},{... | collective-permute-start | bytes 835592 | tf_op jit(solution)/shard_map/ppermute | solution.py:565
  5.3 18.6 %collective-permute-start = (bf16[272,512]{1,0:T(8,128)(2,1)}, bf16[272,512]{1,0:T(8,128)(2,1)}, u32[]{:S(2)}, u32[]{:S(2)}) collective-permute-start(bf16[272,512]{1,0:T(8,128)(2,1)} %pad_maximum_fusion.1), channel_id=1, source_target_pairs={{0,1},{1,2},{3,0},{4,5},{5,6},{7,4},{8,9},{9,10},{11,8},{12,13},{1... | collective-permute-start | bytes 835592 | tf_op jit(solution)/shard_map/ppermute | solution.py:565
  15.0 9.7 %collective-permute-start.2 = (bf16[272,512]{1,0:T(8,128)(2,1)}, bf16[272,512]{1,0:T(8,128)(2,1)}, u32[]{:S(2)}, u32[]{:S(2)}) collective-permute-start(bf16[272,512]{1,0:T(8,128)(2,1)} %pad_maximum_fusion.3), channel_id=1, source_target_pairs={{1,0},{2,1},{3,2},{5,4},{6,5},{7,6},{9,8},{10,9},{11,10},{13,12},{... | collective-permute-start | bytes 835592 | tf_op jit(solution)/shard_map/ppermute | solution.py:565
  39.8 22.8 %collective-permute-start.3 = (bf16[16,192,128]{2,1,0:T(8,128)(2,1)}, bf16[16,192,128]{2,1,0:T(8,128)(2,1)S(1)}, u32[]{:S(2)}, u32[]{:S(2)}) collective-permute-start(bf16[16,192,128]{2,1,0:T(8,128)(2,1)} %get-tuple-element.44), channel_id=1, source_target_pairs={{0,1},{1,0},{2,3},{3,2},{4,5},{5,4},{6,7},{7,6},{8,9},{9,8},{10,11... | collective-permute-start | bytes 2359304 | tf_op jit(solution)/shard_map/ppermute | solution.py:570
  55.4 16.5 %copy-start.9 = (bf16[16,128]{1,0:T(8,128)(2,1)S(1)}, bf16[16,128]{1,0:T(8,128)(2,1)}, u32[]{:S(2)}) copy-start(bf16[16,128]{1,0:T(8,128)(2,1)} %get-tuple-element.42.packet_ref) | copy-start | bytes 12292
  62.6 0.9 copy-start.2
  63.5 8.4 %collective-permute-start.4 = (bf16[16,96,128]{2,1,0:T(8,128)(2,1)}, bf16[16,96,128]{2,1,0:T(8,128)(2,1)S(1)}, u32[]{:S(2)}, u32[]{:S(2)}) collective-permute-start(bf16[16,96,128]{2,1,0:T(8,128)(2,1)} %get-tuple-element.57), channel_id=1, source_target_pairs={{0,1},{1,0},{2,3},{3,2},{4,5},{5,4},{6,7},{7,6},{8,9},{9,8},{10,11... | collective-permute-start | bytes 1179656 | tf_op jit(solution)/shard_map/ppermute | solution.py:570
  71.9 1.1 copy-start.1
  73.1 1.1 copy-start.3
  74.2 1.0 copy-start.5
  82.7 8.9 %collective-permute-start.5 = (bf16[16,96,128]{2,1,0:T(8,128)(2,1)}, bf16[16,96,128]{2,1,0:T(8,128)(2,1)S(1)}, u32[]{:S(2)}, u32[]{:S(2)}) collective-permute-start(bf16[16,96,128]{2,1,0:T(8,128)(2,1)} %get-tuple-element.69), channel_id=1, source_target_pairs={{0,1},{1,0},{2,3},{3,2},{4,5},{5,4},{6,7},{7,6},{8,9},{9,8},{10,11... | collective-permute-start | bytes 1179656 | tf_op jit(solution)/shard_map/ppermute | solution.py:570
  91.6 1.0 copy-start.4
  92.6 0.7 copy-start.8
  93.3 35.7 %copy-start.6 = (f32[1024,2]{0,1:T(2,128)S(1)}, f32[1024,2]{0,1:T(2,128)}, u32[]{:S(2)}) copy-start(f32[1024,2]{0,1:T(2,128)} %param.31) | copy-start | bytes 24580
  93.3 35.7 %copy-start.7 = (s32[8]{0:T(128)S(1)}, s32[8]{0:T(128)}, u32[]{:S(2)}) copy-start(s32[8]{0:T(128)} %stack.27.meta) | copy-start | bytes 100
  153.0 5.3 %collective-permute-start.6 = (f32[104,128]{1,0:T(8,128)S(1)}, f32[104,128]{1,0:T(8,128)S(1)}, u32[]{:S(2)}, u32[]{:S(2)}) collective-permute-start(f32[104,128]{1,0:T(8,128)S(1)} %get-tuple-element.71), channel_id=1, source_target_pairs={{0,1},{1,0},{2,3},{3,2},{4,5},{5,4},{6,7},{7,6},{8,9},{9,8},{10,11... | collective-permute-start | bytes 159752 | tf_op jit(solution)/shard_map/ppermute | solution.py:570

commit v2 on v1

--- a/solution.py
+++ b/solution.py
@@ -2,6 +2,7 @@
 
 import jax
 import jax.numpy as jnp
+import numpy as np
 from jax import lax
 from jax.experimental import pallas as pl
 from jax.experimental.pallas import tpu as pltpu
@@ -63,8 +64,13 @@
                     target[g, place, :] = jnp.concatenate(rows, axis=0).astype(BF16)
 
 
+def own_sample(meta, lengths):
+    own = jnp.minimum(meta[0], SAMPLES - 1)
+    return own, jnp.where(meta[0] < SAMPLES, lengths[own], 0)
+
+
 def forward_kernel(
-    meta, part0, part1, part2, part3, mix_ref, gain_ref, base_ref, dense_ref, heads_ref,
+    meta, lengths, labels, part0, part1, part2, part3, mix_ref, gain_ref, base_ref, bias_ref, dense_ref, heads_ref,
     table_far, wq_far, wk_far, wv_far, wo_far, wp_far,
     q_ref, k_ref, v_ref, do_ref, mixed_ref, normed_ref, lse_ref, delta_ref, own_ref, other_ref,
     packet_ref, logit_ref,
@@ -75,7 +81,7 @@
     near = (table_ref, wq_ref, wk_ref, wv_ref, wo_ref, wp_ref)
     copies = [pltpu.make_async_copy(f, n, sems.at[i]) for i, (f, n) in enumerate(zip(far, near))]
     step = pl.program_id(0)
-    length = meta[1]
+    own, length = own_sample(meta, lengths)
 
     @pl.when(step == 0)
     def _():
@@ -170,16 +176,16 @@
     @pl.when(step == BLOCKS)
     def _():
         span = jnp.maximum(length, 1).astype(F32)
-        dense = dense_ref[...]
-        gate = base_ref[...] + sum_ref[...] / span
+        dense = dense_ref[...].astype(F32)
+        gate = base_ref[...] + bias_ref[...] + sum_ref[...] / span
         crossed = dense + dense * gate
         rows = [dense[:, n * 128 : (n + 1) * 128] for n in range(8)]
         rows += [crossed[:, n * 128 : (n + 1) * 128] for n in range(8)]
         packet_ref[...] = jnp.concatenate(rows, axis=0).astype(BF16)
         a = jnp.sum(crossed * heads_ref[0:1, :], axis=1, keepdims=True)
         c = jnp.sum(crossed * heads_ref[1:2, :], axis=1, keepdims=True)
-        clicked = meta[2].astype(F32)
-        converted = (meta[2] * meta[3]).astype(F32)
+        clicked = labels[own, 0].astype(F32)
+        converted = (labels[own, 0] * labels[own, 1]).astype(F32)
         top = jnp.maximum(jnp.maximum(a, c), 0.0)
         ea, ec = jnp.exp(a - top), jnp.exp(c - top)
         below = jnp.exp(-top) + ea + ec
@@ -226,7 +232,7 @@
 
     @pl.when(step == 2 * BLOCKS - 1)
     def _():
-        spread(meta[6], term_acc, own_ref, other_ref)
+        spread(meta[1], term_acc, own_ref, other_ref)
 
 
 def pair_body(
@@ -271,11 +277,13 @@
 
 def pairs_kernel(
     first,
-    meta, q_ref, k_ref, v_ref, do_ref, lse_ref, delta_ref, logit_ref, prior_ref,
-    mixed_far, normed_far, wq_far, wk_far, wv_far,
-    own_ref, other_ref, sums_ref, packet_ref,
-    dk_acc, dv_acc, kt_ref, term_ref, grad_ref, mixed_ref, normed_ref, wq_ref, wk_ref, wv_ref, sems,
+    meta, lengths, q_ref, k_ref, v_ref, do_ref, lse_ref, delta_ref, logit_ref, *refs
 ):
+    prior_ref = refs[0] if first else None
+    (
+        mixed_far, normed_far, wq_far, wk_far, wv_far, own_ref, other_ref, sums_ref, packet_ref,
+        dk_acc, dv_acc, kt_ref, term_ref, grad_ref, mixed_ref, normed_ref, wq_ref, wk_ref, wv_ref, sems,
+    ) = refs[1:] if first else refs
     step = pl.program_id(0)
     columns = pl.ds(first * 128, 256)
     far = (mixed_far, normed_far) + tuple(w.at[:, columns] for w in (wq_far, wk_far, wv_far))
@@ -287,8 +295,9 @@
         for copy in copies:
             copy.start()
 
+    _, length = own_sample(meta, lengths)
     pair_body(
-        meta[1], q_ref, k_ref, v_ref, do_ref, lse_ref, delta_ref,
+        length, q_ref, k_ref, v_ref, do_ref, lse_ref, delta_ref,
         grad_ref.at[0, step], grad_ref.at[1, step], grad_ref.at[2, step], dk_acc, dv_acc, kt_ref,
     )
 
@@ -303,9 +312,11 @@
             term_ref[n * D : (n + 1) * D, :] = dot(turned, rows)
             part = dot_nt(rows, weight[...])
             total = part if total is None else total + part
-        spread(meta[6], term_ref, own_ref, other_ref)
-        mix = jnp.sum(total, axis=0, keepdims=True) + prior_ref[0:1, :]
-        gain = jnp.sum(total * normed_ref[...].astype(F32), axis=0, keepdims=True) + prior_ref[1:2, :]
+        spread(meta[1], term_ref, own_ref, other_ref)
+        mix = jnp.sum(total, axis=0, keepdims=True)
+        gain = jnp.sum(total * normed_ref[...].astype(F32), axis=0, keepdims=True)
+        if first:
+            mix, gain = mix + prior_ref[0:1, :], gain + prior_ref[1:2, :]
         sums_ref[...] = jnp.concatenate([mix, gain], axis=0)
         logit = logit_ref[...]
         high = logit.astype(BF16).astype(F32)
@@ -353,7 +364,7 @@
     grad_a, grad_c = logits[:, 0:1], logits[:, 1:2]
     lane = lax.broadcasted_iota(jnp.int32, (8, 128), 1)
     line = lax.broadcasted_iota(jnp.int32, (8, 128), 0)
-    picks = jnp.where(lane == meta[7] * 8 + line, 1.0, 0.0).astype(BF16)
+    picks = jnp.where(lane == meta[2] * 8 + line, 1.0, 0.0).astype(BF16)
     dense = [pick(upper_packets, r) for r in range(8)]
     columns = jnp.concatenate([dot_nt(picks, d.astype(BF16)) for d in dense], axis=0)
     flat = [jnp.sum(pick(lower_packets, 4 + r), axis=0, keepdims=True) for r in range(4)]
@@ -385,7 +396,7 @@
 
     for core in (0, 1):
 
-        @pl.when(meta[6] == core)
+        @pl.when(meta[1] == core)
         def _():
             kept_ref[...] = of_core(core)
             sent_ref[...] = of_core(1 - core)
@@ -394,7 +405,7 @@
 def join_kernel(meta, kept_ref, got_ref, sequence_ref, mix_ref, cross_ref, gain_ref, bias_ref, heads_ref):
     for core in (0, 1):
 
-        @pl.when(meta[6] == core)
+        @pl.when(meta[1] == core)
         def _():
             for n in range(2):
                 for ref, owner in ((kept_ref, core), (got_ref, 1 - core)):
@@ -416,7 +427,7 @@
 
 
 def whole(shape):
-    return pl.BlockSpec(shape, lambda i, m: (0,) * len(shape))
+    return pl.BlockSpec(shape, lambda i, *m: (0,) * len(shape))
 
 
 def params(megabytes):
@@ -429,9 +440,9 @@
     return pl.CostEstimate(flops=flops, bytes_accessed=moved, transcendentals=exps)
 
 
-def forward(meta, small, large):
-    early = pl.BlockSpec((BLOCK, D), lambda i, m: (jnp.minimum(i, BLOCKS - 1), 0))
-    late = pl.BlockSpec((BLOCK, D), lambda i, m: (jnp.maximum(i - BLOCKS, 0), 0))
+def forward(scalars, small, large):
+    early = pl.BlockSpec((BLOCK, D), lambda i, *m: (jnp.minimum(i, BLOCKS - 1), 0))
+    late = pl.BlockSpec((BLOCK, D), lambda i, *m: (jnp.maximum(i - BLOCKS, 0), 0))
     outs = [((LEN, D), BF16)] * 6 + [
         ((4, 2, LEN), F32), ((4, 2, LEN), F32), ((16, 192, 128), BF16), ((16, 192, 128), BF16),
         ((16, 128), BF16),
@@ -440,7 +451,7 @@
     return pl.pallas_call(
         forward_kernel,
         grid_spec=pltpu.PrefetchScalarGridSpec(
-            num_scalar_prefetch=1,
+            num_scalar_prefetch=3,
             grid=(2 * BLOCKS,),
             in_specs=[whole(a.shape) for a in small] + [pl.BlockSpec(memory_space=pl.ANY)] * 6,
             out_specs=[early] * 3 + [late] + [early] * 2 + [whole(s) for s, _ in outs[6:]],
@@ -461,20 +472,21 @@
         out_shape=[jax.ShapeDtypeStruct(s, t) for s, t in outs],
         compiler_params=params(58),
         cost_estimate=cost(10**10, 2 * 10**7, 10**7),
-    )(meta, *small, *large)
-
-
-def pairs_back(meta, first, queries, keys, values, grads, lse, delta, logit, prior, *far):
-    lanes = pl.BlockSpec((LEN, 128), lambda i, m: (0, first + i))
-    pair = pl.BlockSpec((1, 2, LEN), lambda i, m: (first + i, 0, 0))
+    )(*scalars, *small, *large)
+
+
+def pairs_back(scalars, first, queries, keys, values, grads, lse, delta, logit, *far):
+    prior = [whole((2, D))] if first else []
+    lanes = pl.BlockSpec((LEN, 128), lambda i, *m: (0, first + i))
+    pair = pl.BlockSpec((1, 2, LEN), lambda i, *m: (first + i, 0, 0))
     outs = [((16, 96, 128), BF16), ((16, 96, 128), BF16), ((2, D), F32), ((16, 128), BF16)]
     return pl.pallas_call(
         functools.partial(pairs_kernel, first),
         grid_spec=pltpu.PrefetchScalarGridSpec(
-            num_scalar_prefetch=1,
+            num_scalar_prefetch=2,
             grid=(2,),
-            in_specs=[lanes] * 4 + [pair] * 2 + [whole(logit.shape), whole(prior.shape)]
-            + [pl.BlockSpec(memory_space=pl.ANY)] * 5,
+            in_specs=[lanes] * 4 + [pair] * 2 + [whole(logit.shape)]
+            + prior + [pl.BlockSpec(memory_space=pl.ANY)] * 5,
             out_specs=[whole(s) for s, _ in outs],
             scratch_shapes=[
                 pltpu.VMEM((LEN, 128), F32),
@@ -489,7 +501,7 @@
         out_shape=[jax.ShapeDtypeStruct(s, t) for s, t in outs],
         compiler_params=params(60),
         cost_estimate=cost(10**10, 10**7, 4 * 10**6),
-    )(meta, queries, keys, values, grads, lse, delta, logit, prior, *far)
+    )(*scalars, queries, keys, values, grads, lse, delta, logit, *far)
 
 
 def cut_pieces(packet, *halves):
@@ -575,35 +587,30 @@
     w_key, w_value, w_out, w_pool, w_cross, b_cross, w_heads,
 ):
     me = lax.axis_index(CTX)
-    core = lax.axis_index("core")
-    chip = lax.axis_index(("z", "ylo", "x", "yhi"))
     own = jnp.minimum(me, SAMPLES - 1)
     parts = to_samples(event_ids, event_side, me)
-    length = jnp.where(me < SAMPLES, lengths[own], 0)
-    plane = lax.axis_index(PLANE)
-    meta = [me, length, labels[own, 0], labels[own, 1], chip, lax.axis_index("z"), core, plane]
-    meta = jnp.stack(meta).astype(jnp.int32)
+    device = np.arange(256)
+    places = np.stack([device % 4, device % 2, device // 2 % 16] + [0 * device] * 5, axis=1)
+    meta = jnp.asarray(places, jnp.int32)[lax.axis_index(("z", "ylo", "x") + CTX)]
     dense = lax.dynamic_slice_in_dim(dense_input, own, 1, 0)
     mix_row = dot(dense, w_mix)
-    base = dot(dense, w_cross) + b_cross[None]
-
+    base = dot(dense, w_cross)
     heads = w_heads.T
     (queries, keys, values, grads, mixed, normed, lse, delta, own, other, packet, logit) = forward(
-        meta,
-        (*parts, mix_row, seq_gain[None], base, dense.astype(F32), heads),
+        (meta, lengths, labels),
+        (*parts, mix_row, seq_gain[None], base, b_cross[None], dense, heads),
         (event_table, w_query, w_key, w_value, w_out, w_pool),
     )
     got = swap_cores(other)
     attention = (queries, keys, values, grads, lse, delta, logit)
     rest = (mixed, normed, w_query, w_key, w_value)
-    own_first, other_first, sums, _ = pairs_back(
-        meta, 0, *attention, jnp.zeros((2, D), F32), *rest
-    )
+    own_first, other_first, sums, _ = pairs_back((meta, lengths), 0, *attention, *rest)
     got, other_first = lax.optimization_barrier((got, other_first))
     pieces = cut_pieces(packet, own, got, own_first, swap_cores(other_first))
     pieces, attention = lax.optimization_barrier((pieces, attention))
     upper_plane = lax.all_to_all(pieces, PLANE, 0, 0)
-    own, other, _, packet = pairs_back(meta, 2, *attention, sums, *rest)
+    own, other, _, packet = pairs_back((meta, lengths), 2, *attention, sums, *rest)
+    upper_plane, other = lax.optimization_barrier((upper_plane, other))
     pieces = cut_pieces(packet, own, swap_cores(other))
     lower_plane = lax.all_to_all(pieces, PLANE, 0, 0)
     got = lax.all_to_all(sum_pieces(meta, upper_plane, lower_plane, heads), "z", 0, 0)

time: 161 us -> 148 us (0.919)
  blocking collectives: 57.5 us -> 33.2 us
  waiting for transfers between devices: 4.72 us -> 20.2 us
  local copies, waits for them, and re-layouts: 11.1 us -> 7.21 us
    all_to_all x1 -> x0, blocking collectives: 21.3 us -> none  [per_device(): upper_plane = lax.all_to_all(pieces, PLANE, 0, 0)]
    all_to_all x0 -> x1, waiting for transfers between devices: none -> 12.9 us  [per_device(): upper_plane = lax.all_to_all(pieces, PLANE, 0, 0)]
    all_to_all x0 -> x1, starting transfers between devices: none -> 8.06 us  [per_device(): upper_plane = lax.all_to_all(pieces, PLANE, 0, 0)]
    ppermute x4, starting transfers between devices: 33.7 us -> 26.5 us  [swap_cores(): return lax.ppermute(value, 'core', [(0, 1), (1, 0)])]
    all_to_all x1, blocking collectives: 21.9 us -> 18.9 us  [per_device(): lax.all_to_all(sum_pieces(meta, upper_plane, lower_plane, heads), 'z', 0, 0)]
    ppermute x3, waiting for transfers between devices: 0.71 us -> 3.25 us  [to_samples(): got.append(lax.ppermute(part((me + k) % 4), CTX, pairs))]
    another operation x1 -> x0, local copies, waits for them, and re-layouts: 1.93 us -> none  [per_device(): meta = jnp.stack(meta).astype(jnp.int32)]
    unnamed x34 -> x31, local copies, waits for them, and re-layouts: 5.91 us -> 4.46 us
  transfers between devices with their start and end apart: 7 -> 8, of which waited for: 4 -> 5; matrix products, arithmetic and copies ran while one was open for 5% -> 4% of each run, Pallas kernels for 4% -> 10%
where the time goes in v2:
time: 148 us; the launch traced here: 147 us
  starting transfers between devices  46.7 us (32%)
  blocking collectives  33.2 us (22%)
  Pallas kernels  33.1 us (22%)
  waiting for transfers between devices  20.2 us (14%)
  local copies, waits for them, and re-layouts  7.21 us (5%)
  other arithmetic  3.78 us (3%)
  matrix products  1.81 us (1%)
    ppermute x4, starting transfers between devices, swap_cores(): return lax.ppermute(value, 'core', [(0, 1), (1, 0)])  26.5 us
    all_to_all x1, blocking collectives, per_device(): lax.all_to_all(sum_pieces(meta, upper_plane, lower_plane, heads), 'z', 0, 0)  18.9 us
    pallas_call x1, Pallas kernels, forward(): pl.pallas_call(forward_kernel, grid_spec=pltpu.PrefetchScalarGridSpec(num...  15.2 us
    all_to_all x1, blocking collectives, per_device(): lower_plane = lax.all_to_all(pieces, PLANE, 0, 0)  14.3 us
    pallas_call x2, Pallas kernels, pairs_back(): pl.pallas_call(functools.partial(pairs_kernel, first), grid_spec=pltpu.Pr...  14.3 us
    all_to_all x1, waiting for transfers between devices, per_device(): upper_plane = lax.all_to_all(pieces, PLANE, 0, 0)  12.9 us
    ppermute x3, starting transfers between devices, to_samples(): got.append(lax.ppermute(part((me + k) % 4), CTX, pairs))  12.1 us
    all_to_all x1, starting transfers between devices, per_device(): upper_plane = lax.all_to_all(pieces, PLANE, 0, 0)  8.06 us
  transfers between devices with their start and end apart: 8, of which 5 were waited for; matrix products, arithmetic and copies ran while one was open for 4% of the time, Pallas kernels for 10%

profile of v2, /device:TPU:1, one launch (start us, length us, event | category | flops | bytes accessed | tf_op | source)
XLA Modules:
  0.0 147.1 jit_solution(18346111144417000356)
XLA Ops:
  0.7 0.8 fusion.11
  1.8 1.4 dynamic-slice_bitcast_fusion
  3.2 0.7 pad_maximum_fusion.2
  3.9 1.3 collective-permute-start.1
  5.2 0.7 pad_maximum_fusion.1
  5.9 8.9 %collective-permute-start = (bf16[272,512]{1,0:T(8,128)(2,1)}, bf16[272,512]{1,0:T(8,128)(2,1)}, u32[]{:S(2)}, u32[]{:S(2)}) collective-permute-start(bf16[272,512]{1,0:T(8,128)(2,1)} %pad_maximum_fusion.1), channel_id=1, source_target_pairs={{0,1},{1,2},{3,0},{4,5},{5,6},{7,4},{8,9},{9,10},{11,8},{12,13},{1... | collective-permute-start | bytes 835592 | tf_op jit(solution)/shard_map/ppermute | solution.py:577
  14.8 0.7 pad_maximum_fusion.3
  15.6 1.9 %collective-permute-start.2 = (bf16[272,512]{1,0:T(8,128)(2,1)}, bf16[272,512]{1,0:T(8,128)(2,1)}, u32[]{:S(2)}, u32[]{:S(2)}) collective-permute-start(bf16[272,512]{1,0:T(8,128)(2,1)} %pad_maximum_fusion.3), channel_id=1, source_target_pairs={{1,0},{2,1},{3,2},{5,4},{6,5},{7,6},{9,8},{10,9},{11,10},{13,12},{... | collective-permute-start | bytes 835592 | tf_op jit(solution)/shard_map/ppermute | solution.py:577
  17.6 0.8 fusion.7.mix_ref
  18.4 0.7 pad_maximum_fusion.part0
  19.1 1.2 fusion.12.meta
  21.0 1.0 fusion.5.base_ref
  22.0 3.2 %collective-permute-done.2.part3 = bf16[272,512]{1,0:T(8,128)(2,1)} collective-permute-done((bf16[272,512]{1,0:T(8,128)(2,1)}, bf16[272,512]{1,0:T(8,128)(2,1)}, u32[]{:S(2)}, u32[]{:S(2)}) %collective-permute-start.2) | collective-permute-done | bytes 278560 | tf_op jit(solution)/shard_map/ppermute | solution.py:577
  25.2 15.2 %shard_map.208 = (bf16[1024,512]{1,0:T(8,128)(2,1)}, bf16[1024,512]{1,0:T(8,128)(2,1)}, bf16[1024,512]{1,0:T(8,128)(2,1)}, bf16[1024,512]{1,0:T(8,128)(2,1)}, bf...) custom-call(s32[8]{0:T(128)} %fusion.12.meta, ...), custom_call_target="tpu_custom_call" | custom-call | flops 10000000000 | bytes 20000000 | tf_op jit(solution)/shard_map/pallas_call | solution.py:451
  40.5 13.6 %collective-permute-start.3 = (bf16[16,192,128]{2,1,0:T(8,128)(2,1)}, bf16[16,192,128]{2,1,0:T(8,128)(2,1)S(1)}, u32[]{:S(2)}, u32[]{:S(2)}) collective-permute-start(bf16[16,192,128]{2,1,0:T(8,128)(2,1)} %get-tuple-element.46), channel_id=1, source_target_pairs={{0,1},{1,0},{2,3},{3,2},{4,5},{5,4},{6,7},{7,6},{8,9},{9,8},{10,11... | collective-permute-start | bytes 2359304 | tf_op jit(solution)/shard_map/ppermute | solution.py:582
  54.1 7.1 %shard_map.209 = (bf16[16,96,128]{2,1,0:T(8,128)(2,1)}, bf16[16,96,128]{2,1,0:T(8,128)(2,1)}, f32[2,512]{1,0:T(2,128)}, bf16[16,128]{1,0:T(8,128)(2,1)}) custom-call(s32[8]{0:T(128)} %fusion.12.meta, s32[3]{0:T(128)} %lengths.5, bf16[1024,512]{1,0:T(8,128)(2,1)} %get-tuple-element.61.q_ref, bf16[1024,512]{1,0:T(8,128)(2,1)} %get-tuple-element.62.k_ref, ...), custom_call_target="tpu_custom_call" | custom-call | flops 10000000000 | bytes 10000000 | tf_op jit(solution)/shard_map/pallas_call | solution.py:483
  61.3 7.0 %collective-permute-start.4 = (bf16[16,96,128]{2,1,0:T(8,128)(2,1)}, bf16[16,96,128]{2,1,0:T(8,128)(2,1)S(1)}, u32[]{:S(2)}, u32[]{:S(2)}) collective-permute-start(bf16[16,96,128]{2,1,0:T(8,128)(2,1)} %get-tuple-element.59), channel_id=1, source_target_pairs={{0,1},{1,0},{2,3},{3,2},{4,5},{5,4},{6,7},{7,6},{8,9},{9,8},{10,11... | collective-permute-start | bytes 1179656 | tf_op jit(solution)/shard_map/ppermute | solution.py:582
  68.3 1.6 %collective-permute-done.4.refs_3_ = bf16[16,96,128]{2,1,0:T(8,128)(2,1)S(1)} collective-permute-done((bf16[16,96,128]{2,1,0:T(8,128)(2,1)}, bf16[16,96,128]{2,1,0:T(8,128)(2,1)S(1)}, u32[]{:S(2)}, u32[]{:S(2)}) %collective-permute-start.4) | collective-permute-done | bytes 393248 | tf_op jit(solution)/shard_map/ppermute | solution.py:582
  69.9 1.0 copy-done.4
  71.1 1.0 copy-done.1
  72.2 8.1 %all-to-all-start = ((bf16[16,304,128]{2,1,0:T(8,128)(2,1)}), bf16[16,304,128]{2,1,0:T(8,128)(2,1)S(1)}, u32[]{:S(2)}, u32[]{:S(2)}) async-start(bf16[16,304,128]{2,1,0:T(8,128)(2,1)} %copy-done.1), calls=%async_computation | async-start | bytes 2490368 | tf_op jit(solution)/shard_map/all_to_all | solution.py:611
  80.3 7.1 %shard_map.211 = (bf16[16,96,128]{2,1,0:T(8,128)(2,1)}, bf16[16,96,128]{2,1,0:T(8,128)(2,1)}, f32[2,512]{1,0:T(2,128)}, bf16[16,128]{1,0:T(8,128)(2,1)}) custom-call(s32[8]{0:T(128)} %fusion.12.meta, s32[3]{0:T(128)} %lengths.5, bf16[1024,512]{1,0:T(8,128)(2,1)} %get-tuple-element.61.q_ref, bf16[1024,512]{1,0:T(8,128)(2,1)} %get-tuple-element.62.k_ref, ...), custom_call_target="tpu_custom_call" | custom-call | flops 10000000000 | bytes 10000000 | tf_op jit(solution)/shard_map/pallas_call | solution.py:483
  87.4 12.9 %all-to-all-done.upper_ref = bf16[16,304,128]{2,1,0:T(8,128)(2,1)S(1)} async-done(((bf16[16,304,128]{2,1,0:T(8,128)(2,1)}), bf16[16,304,128]{2,1,0:T(8,128)(2,1)S(1)}, u32[]{:S(2)}, u32[]{:S(2)}) %all-to-all-start) | async-done | bytes 1245216 | tf_op jit(solution)/shard_map/all_to_all | solution.py:611
  100.3 2.0 %collective-permute-start.5 = (bf16[16,96,128]{2,1,0:T(8,128)(2,1)}, bf16[16,96,128]{2,1,0:T(8,128)(2,1)S(1)}, u32[]{:S(2)}, u32[]{:S(2)}) collective-permute-start(bf16[16,96,128]{2,1,0:T(8,128)(2,1)} %get-tuple-element.73), channel_id=1, source_target_pairs={{0,1},{1,0},{2,3},{3,2},{4,5},{5,4},{6,7},{7,6},{8,9},{9,8},{10,11... | collective-permute-start | bytes 1179656 | tf_op jit(solution)/shard_map/ppermute | solution.py:582
  102.3 1.6 %collective-permute-done.5.refs_1_ = bf16[16,96,128]{2,1,0:T(8,128)(2,1)S(1)} collective-permute-done((bf16[16,96,128]{2,1,0:T(8,128)(2,1)}, bf16[16,96,128]{2,1,0:T(8,128)(2,1)S(1)}, u32[]{:S(2)}, u32[]{:S(2)}) %collective-permute-start.5) | collective-permute-done | bytes 393248 | tf_op jit(solution)/shard_map/ppermute | solution.py:582
  103.9 1.0 copy-done.3
  105.7 14.3 %all_to_all.15.lower_ref = bf16[16,112,128]{2,1,0:T(8,128)(2,1)S(1)} all-to-all(bf16[16,112,128]{2,1,0:T(8,128)(2,1)S(1)} %shard_map.212), channel_id=1, replica_groups=mesh['z'=8,'ylo'=2,'x'=4,'yhi'=2,'core'=2] {'ylo','x','yhi'}, dimensions={0} | all-to-all | bytes 917504 | tf_op jit(solution)/shard_map/all_to_all | solution.py:615
  120.0 1.4 shard_map.213
  121.4 18.9 %all_to_all.16.got_ref = bf16[8,176,128]{2,1,0:T(8,128)(2,1)S(1)} all-to-all(bf16[8,176,128]{2,1,0:T(8,128)(2,1)S(1)} %shard_map.213), channel_id=1, replica_groups=mesh['z'=8,'ylo'=2,'x'=4,'yhi'=2,'core'=2] {'z'}, dimensions={0} | all-to-all | bytes 720896 | tf_op jit(solution)/shard_map/all_to_all | solution.py:616
  140.9 3.8 %collective-permute-start.6 = (f32[104,128]{1,0:T(8,128)S(1)}, f32[104,128]{1,0:T(8,128)S(1)}, u32[]{:S(2)}, u32[]{:S(2)}) collective-permute-start(f32[104,128]{1,0:T(8,128)S(1)} %get-tuple-element.75), channel_id=1, source_target_pairs={{0,1},{1,0},{2,3},{3,2},{4,5},{5,4},{6,7},{7,6},{8,9},{9,8},{10,11... | collective-permute-start | bytes 159752 | tf_op jit(solution)/shard_map/ppermute | solution.py:582
  144.8 0.9 collective-permute-done.6.got_ref
  145.6 1.2 shard_map.215
  (37 shorter events, 2.6 us)
Async XLA Ops:
  0.6 20.4 %copy-start = (bf16[1024,1024]{1,0:T(8,128)(2,1)S(1)}, bf16[1024,1024]{1,0:T(8,128)(2,1)}, u32[]{:S(2)}) copy-start(bf16[1024,1024]{1,0:T(8,128)(2,1)} %param.30) | copy-start | bytes 6291460
  1.6 15.9 %copy-start.11 = (bf16[3,1024]{1,0:T(4,128)(2,1)S(1)}, bf16[3,1024]{1,0:T(4,128)(2,1)}, u32[]{:S(2)}) copy-start(bf16[3,1024]{1,0:T(4,128)(2,1)} %param.20) | copy-start | bytes 18436
  1.6 16.0 %copy-start.9 = (bf16[1024,512]{1,0:T(8,128)(2,1)S(1)}, bf16[1024,512]{1,0:T(8,128)(2,1)}, u32[]{:S(2)}) copy-start(bf16[1024,512]{1,0:T(8,128)(2,1)} %param.24) | copy-start | bytes 3145732
  3.1 17.2 %copy-start.12 = (s32[3,2]{0,1:T(2,128)S(1)}, s32[3,2]{0,1:T(2,128)}, u32[]{:S(2)}) copy-start(s32[3,2]{0,1:T(2,128)} %param.21) | copy-start | bytes 76
  3.9 18.1 %collective-permute-start.1 = (bf16[272,512]{1,0:T(8,128)(2,1)}, bf16[272,512]{1,0:T(8,128)(2,1)}, u32[]{:S(2)}, u32[]{:S(2)}) collective-permute-start(bf16[272,512]{1,0:T(8,128)(2,1)} %pad_maximum_fusion.2), channel_id=1, source_target_pairs={{0,2},{2,0},{3,1},{4,6},{6,4},{7,5},{8,10},{10,8},{11,9},{12,14},{... | collective-permute-start | bytes 835592 | tf_op jit(solution)/shard_map/ppermute | solution.py:577
  5.9 16.1 %collective-permute-start = (bf16[272,512]{1,0:T(8,128)(2,1)}, bf16[272,512]{1,0:T(8,128)(2,1)}, u32[]{:S(2)}, u32[]{:S(2)}) collective-permute-start(bf16[272,512]{1,0:T(8,128)(2,1)} %pad_maximum_fusion.1), channel_id=1, source_target_pairs={{0,1},{1,2},{3,0},{4,5},{5,6},{7,4},{8,9},{9,10},{11,8},{12,13},{1... | collective-permute-start | bytes 835592 | tf_op jit(solution)/shard_map/ppermute | solution.py:577
  15.6 9.7 %collective-permute-start.2 = (bf16[272,512]{1,0:T(8,128)(2,1)}, bf16[272,512]{1,0:T(8,128)(2,1)}, u32[]{:S(2)}, u32[]{:S(2)}) collective-permute-start(bf16[272,512]{1,0:T(8,128)(2,1)} %pad_maximum_fusion.3), channel_id=1, source_target_pairs={{1,0},{2,1},{3,2},{5,4},{6,5},{7,6},{9,8},{10,9},{11,10},{13,12},{... | collective-permute-start | bytes 835592 | tf_op jit(solution)/shard_map/ppermute | solution.py:577
  17.5 7.7 %copy-start.10 = (bf16[1,1024]{1,0:T(2,128)(2,1)}, bf16[1,1024]{1,0:T(2,128)(2,1)S(1)}, u32[]{:S(2)}) copy-start(bf16[1,1024]{1,0:T(2,128)(2,1)S(1)} %constant_dynamic-slice_fusion.dense_ref) | copy-start | bytes 6148
  40.5 20.8 %collective-permute-start.3 = (bf16[16,192,128]{2,1,0:T(8,128)(2,1)}, bf16[16,192,128]{2,1,0:T(8,128)(2,1)S(1)}, u32[]{:S(2)}, u32[]{:S(2)}) collective-permute-start(bf16[16,192,128]{2,1,0:T(8,128)(2,1)} %get-tuple-element.46), channel_id=1, source_target_pairs={{0,1},{1,0},{2,3},{3,2},{4,5},{5,4},{6,7},{7,6},{8,9},{9,8},{10,11... | collective-permute-start | bytes 2359304 | tf_op jit(solution)/shard_map/ppermute | solution.py:582
  54.1 15.7 %copy-start.2 = (bf16[16,192,128]{2,1,0:T(8,128)(2,1)S(1)}, bf16[16,192,128]{2,1,0:T(8,128)(2,1)}, u32[]{:S(2)}) copy-start(bf16[16,192,128]{2,1,0:T(8,128)(2,1)} %get-tuple-element.45.refs_0_) | copy-start | bytes 2359300
  54.1 15.7 %copy-start.8 = (bf16[16,128]{1,0:T(8,128)(2,1)S(1)}, bf16[16,128]{1,0:T(8,128)(2,1)}, u32[]{:S(2)}) copy-start(bf16[16,128]{1,0:T(8,128)(2,1)} %get-tuple-element.44.packet_ref) | copy-start | bytes 12292
  61.3 8.6 %collective-permute-start.4 = (bf16[16,96,128]{2,1,0:T(8,128)(2,1)}, bf16[16,96,128]{2,1,0:T(8,128)(2,1)S(1)}, u32[]{:S(2)}, u32[]{:S(2)}) collective-permute-start(bf16[16,96,128]{2,1,0:T(8,128)(2,1)} %get-tuple-element.59), channel_id=1, source_target_pairs={{0,1},{1,0},{2,3},{3,2},{4,5},{5,4},{6,7},{7,6},{8,9},{9,8},{10,11... | collective-permute-start | bytes 1179656 | tf_op jit(solution)/shard_map/ppermute | solution.py:582
  69.9 1.0 copy-start.4
  71.1 1.0 copy-start.1
  72.2 28.1 %all-to-all-start = ((bf16[16,304,128]{2,1,0:T(8,128)(2,1)}), bf16[16,304,128]{2,1,0:T(8,128)(2,1)S(1)}, u32[]{:S(2)}, u32[]{:S(2)}) async-start(bf16[16,304,128]{2,1,0:T(8,128)(2,1)} %copy-done.1), calls=%async_computation | async-start | bytes 2490368 | tf_op jit(solution)/shard_map/all_to_all | solution.py:611
  80.2 39.7 %copy-start.5 = (f32[1024,2]{0,1:T(2,128)S(1)}, f32[1024,2]{0,1:T(2,128)}, u32[]{:S(2)}) copy-start(f32[1024,2]{0,1:T(2,128)} %param.32) | copy-start | bytes 24580
  87.4 32.6 %copy-start.6 = (s32[8]{0:T(128)S(1)}, s32[8]{0:T(128)}, u32[]{:S(2)}) copy-start(s32[8]{0:T(128)} %fusion.12.meta) | copy-start | bytes 100
  100.3 3.6 %collective-permute-start.5 = (bf16[16,96,128]{2,1,0:T(8,128)(2,1)}, bf16[16,96,128]{2,1,0:T(8,128)(2,1)S(1)}, u32[]{:S(2)}, u32[]{:S(2)}) collective-permute-start(bf16[16,96,128]{2,1,0:T(8,128)(2,1)} %get-tuple-element.73), channel_id=1, source_target_pairs={{0,1},{1,0},{2,3},{3,2},{4,5},{5,4},{6,7},{7,6},{8,9},{9,8},{10,11... | collective-permute-start | bytes 1179656 | tf_op jit(solution)/shard_map/ppermute | solution.py:582
  103.9 1.0 copy-start.3
  104.9 0.7 copy-start.7
  140.9 4.7 %collective-permute-start.6 = (f32[104,128]{1,0:T(8,128)S(1)}, f32[104,128]{1,0:T(8,128)S(1)}, u32[]{:S(2)}, u32[]{:S(2)}) collective-permute-start(f32[104,128]{1,0:T(8,128)S(1)} %get-tuple-element.75), channel_id=1, source_target_pairs={{0,1},{1,0},{2,3},{3,2},{4,5},{5,4},{6,7},{7,6},{8,9},{9,8},{10,11... | collective-permute-start | bytes 159752 | tf_op jit(solution)/shard_map/ppermute | solution.py:582

commit v3 on v2

--- a/solution.py
+++ b/solution.py
@@ -610,8 +610,8 @@
     pieces, attention = lax.optimization_barrier((pieces, attention))
     upper_plane = lax.all_to_all(pieces, PLANE, 0, 0)
     own, other, _, packet = pairs_back((meta, lengths), 2, *attention, sums, *rest)
-    upper_plane, other = lax.optimization_barrier((upper_plane, other))
     pieces = cut_pieces(packet, own, swap_cores(other))
+    upper_plane, pieces = lax.optimization_barrier((upper_plane, pieces))
     lower_plane = lax.all_to_all(pieces, PLANE, 0, 0)
     got = lax.all_to_all(sum_pieces(meta, upper_plane, lower_plane, heads), "z", 0, 0)
     kept, sent = total_rows(meta, got)

time: 148 us -> 143 us (0.966)
  waiting for transfers between devices: 20.2 us -> 8.78 us
  starting transfers between devices: 46.7 us -> 50.3 us
  blocking collectives: 33.2 us -> 35.6 us
    all_to_all x1, waiting for transfers between devices: 12.9 us -> 1.53 us  [per_device(): upper_plane = lax.all_to_all(pieces, PLANE, 0, 0)]
    ppermute x4, starting transfers between devices: 26.5 us -> 32.5 us  [swap_cores(): return lax.ppermute(value, 'core', [(0, 1), (1, 0)])]
    all_to_all x1, blocking collectives: 18.9 us -> 21.2 us  [per_device(): lax.all_to_all(sum_pieces(meta, upper_plane, lower_plane, heads), 'z', 0, 0)]
    all_to_all x1, starting transfers between devices: 8.06 us -> 5.76 us  [per_device(): upper_plane = lax.all_to_all(pieces, PLANE, 0, 0)]
    unnamed x31 -> x33, local copies, waits for them, and re-layouts: 4.46 us -> 5.22 us
where the time goes in v3:
time: 143 us
  starting transfers between devices  50.3 us (35%)
  blocking collectives  35.6 us (25%)
  Pallas kernels  33 us (23%)
  waiting for transfers between devices  8.78 us (6%)
  local copies, waits for them, and re-layouts  7.98 us (6%)
  other arithmetic  3.77 us (3%)
  matrix products  1.81 us (1%)
    ppermute x4, starting transfers between devices, swap_cores(): return lax.ppermute(value, 'core', [(0, 1), (1, 0)])  32.5 us
    all_to_all x1, blocking collectives, per_device(): lax.all_to_all(sum_pieces(meta, upper_plane, lower_plane, heads), 'z', 0, 0)  21.2 us
    pallas_call x1, Pallas kernels, forward(): pl.pallas_call(forward_kernel, grid_spec=pltpu.PrefetchScalarGridSpec(num...  15.2 us
    all_to_all x1, blocking collectives, per_device(): lower_plane = lax.all_to_all(pieces, PLANE, 0, 0)  14.4 us
    pallas_call x2, Pallas kernels, pairs_back(): pl.pallas_call(functools.partial(pairs_kernel, first), grid_spec=pltpu.Pr...  14.2 us
    ppermute x3, starting transfers between devices, to_samples(): got.append(lax.ppermute(part((me + k) % 4), CTX, pairs))  12.1 us
    all_to_all x1, starting transfers between devices, per_device(): upper_plane = lax.all_to_all(pieces, PLANE, 0, 0)  5.76 us
    unnamed x33, local copies, waits for them, and re-layouts  5.22 us
  transfers between devices with their start and end apart: 8, of which 5 were waited for; matrix products, arithmetic and copies ran while one was open for 4% of the time, Pallas kernels for 10%

profile of v3, /device:TPU:1, one launch (start us, length us, event | category | flops | bytes accessed | tf_op | source)
XLA Modules:
  0.0 142.5 jit_solution(4575421172360562264)
XLA Ops:
  0.7 0.8 fusion.11
  1.8 1.4 dynamic-slice_bitcast_fusion
  3.9 1.3 collective-permute-start.1
  5.2 0.7 pad_maximum_fusion.1
  5.9 8.9 %collective-permute-start = (bf16[272,512]{1,0:T(8,128)(2,1)}, bf16[272,512]{1,0:T(8,128)(2,1)}, u32[]{:S(2)}, u32[]{:S(2)}) collective-permute-start(bf16[272,512]{1,0:T(8,128)(2,1)} %pad_maximum_fusion.1), channel_id=1, source_target_pairs={{0,1},{1,2},{3,0},{4,5},{5,6},{7,4},{8,9},{9,10},{11,8},{12,13},{1... | collective-permute-start | bytes 835592 | tf_op jit(solution)/shard_map/ppermute | solution.py:577
  14.8 0.7 pad_maximum_fusion.3
  15.6 1.9 %collective-permute-start.2 = (bf16[272,512]{1,0:T(8,128)(2,1)}, bf16[272,512]{1,0:T(8,128)(2,1)}, u32[]{:S(2)}, u32[]{:S(2)}) collective-permute-start(bf16[272,512]{1,0:T(8,128)(2,1)} %pad_maximum_fusion.3), channel_id=1, source_target_pairs={{1,0},{2,1},{3,2},{5,4},{6,5},{7,6},{9,8},{10,9},{11,10},{13,12},{... | collective-permute-start | bytes 835592 | tf_op jit(solution)/shard_map/ppermute | solution.py:577
  17.6 0.8 fusion.7.mix_ref
  18.4 0.7 pad_maximum_fusion.part0
  19.1 1.2 fusion.12.meta
  21.0 1.0 fusion.5.base_ref
  22.0 3.2 %collective-permute-done.2.part3 = bf16[272,512]{1,0:T(8,128)(2,1)} collective-permute-done((bf16[272,512]{1,0:T(8,128)(2,1)}, bf16[272,512]{1,0:T(8,128)(2,1)}, u32[]{:S(2)}, u32[]{:S(2)}) %collective-permute-start.2) | collective-permute-done | bytes 278560 | tf_op jit(solution)/shard_map/ppermute | solution.py:577
  25.2 15.2 %shard_map.208 = (bf16[1024,512]{1,0:T(8,128)(2,1)}, bf16[1024,512]{1,0:T(8,128)(2,1)}, bf16[1024,512]{1,0:T(8,128)(2,1)}, bf16[1024,512]{1,0:T(8,128)(2,1)}, bf...) custom-call(s32[8]{0:T(128)} %fusion.12.meta, ...), custom_call_target="tpu_custom_call" | custom-call | flops 10000000000 | bytes 20000000 | tf_op jit(solution)/shard_map/pallas_call | solution.py:451
  40.5 13.6 %collective-permute-start.3 = (bf16[16,192,128]{2,1,0:T(8,128)(2,1)}, bf16[16,192,128]{2,1,0:T(8,128)(2,1)S(1)}, u32[]{:S(2)}, u32[]{:S(2)}) collective-permute-start(bf16[16,192,128]{2,1,0:T(8,128)(2,1)} %get-tuple-element.46), channel_id=1, source_target_pairs={{0,1},{1,0},{2,3},{3,2},{4,5},{5,4},{6,7},{7,6},{8,9},{9,8},{10,11... | collective-permute-start | bytes 2359304 | tf_op jit(solution)/shard_map/ppermute | solution.py:582
  54.1 7.1 %shard_map.209 = (bf16[16,96,128]{2,1,0:T(8,128)(2,1)}, bf16[16,96,128]{2,1,0:T(8,128)(2,1)}, f32[2,512]{1,0:T(2,128)}, bf16[16,128]{1,0:T(8,128)(2,1)}) custom-call(s32[8]{0:T(128)} %fusion.12.meta, s32[3]{0:T(128)} %lengths.5, bf16[1024,512]{1,0:T(8,128)(2,1)} %get-tuple-element.61.q_ref, bf16[1024,512]{1,0:T(8,128)(2,1)} %get-tuple-element.62.k_ref, ...), custom_call_target="tpu_custom_call" | custom-call | flops 10000000000 | bytes 10000000 | tf_op jit(solution)/shard_map/pallas_call | solution.py:483
  61.3 7.0 %collective-permute-start.4 = (bf16[16,96,128]{2,1,0:T(8,128)(2,1)}, bf16[16,96,128]{2,1,0:T(8,128)(2,1)S(1)}, u32[]{:S(2)}, u32[]{:S(2)}) collective-permute-start(bf16[16,96,128]{2,1,0:T(8,128)(2,1)} %get-tuple-element.59), channel_id=1, source_target_pairs={{0,1},{1,0},{2,3},{3,2},{4,5},{5,4},{6,7},{7,6},{8,9},{9,8},{10,11... | collective-permute-start | bytes 1179656 | tf_op jit(solution)/shard_map/ppermute | solution.py:582
  68.3 1.6 %collective-permute-done.4.refs_3_ = bf16[16,96,128]{2,1,0:T(8,128)(2,1)S(1)} collective-permute-done((bf16[16,96,128]{2,1,0:T(8,128)(2,1)}, bf16[16,96,128]{2,1,0:T(8,128)(2,1)S(1)}, u32[]{:S(2)}, u32[]{:S(2)}) %collective-permute-start.4) | collective-permute-done | bytes 393248 | tf_op jit(solution)/shard_map/ppermute | solution.py:582
  69.9 1.0 copy-done.5
  71.1 1.0 copy-done.1
  72.2 5.8 %all-to-all-start = ((bf16[16,304,128]{2,1,0:T(8,128)(2,1)}), bf16[16,304,128]{2,1,0:T(8,128)(2,1)S(1)}, u32[]{:S(2)}, u32[]{:S(2)}) async-start(bf16[16,304,128]{2,1,0:T(8,128)(2,1)} %copy-done.1), calls=%async_computation | async-start | bytes 2490368 | tf_op jit(solution)/shard_map/all_to_all | solution.py:611
  77.9 7.1 %shard_map.211 = (bf16[16,96,128]{2,1,0:T(8,128)(2,1)}, bf16[16,96,128]{2,1,0:T(8,128)(2,1)}, f32[2,512]{1,0:T(2,128)}, bf16[16,128]{1,0:T(8,128)(2,1)}) custom-call(s32[8]{0:T(128)} %fusion.12.meta, s32[3]{0:T(128)} %lengths.5, bf16[1024,512]{1,0:T(8,128)(2,1)} %get-tuple-element.61.q_ref, bf16[1024,512]{1,0:T(8,128)(2,1)} %get-tuple-element.62.k_ref, ...), custom_call_target="tpu_custom_call" | custom-call | flops 10000000000 | bytes 10000000 | tf_op jit(solution)/shard_map/pallas_call | solution.py:483
  85.1 7.4 %collective-permute-start.5 = (bf16[16,96,128]{2,1,0:T(8,128)(2,1)}, bf16[16,96,128]{2,1,0:T(8,128)(2,1)S(1)}, u32[]{:S(2)}, u32[]{:S(2)}) collective-permute-start(bf16[16,96,128]{2,1,0:T(8,128)(2,1)} %get-tuple-element.71), channel_id=1, source_target_pairs={{0,1},{1,0},{2,3},{3,2},{4,5},{5,4},{6,7},{7,6},{8,9},{9,8},{10,11... | collective-permute-start | bytes 1179656 | tf_op jit(solution)/shard_map/ppermute | solution.py:582
  92.5 1.6 %collective-permute-done.5.refs_1_ = bf16[16,96,128]{2,1,0:T(8,128)(2,1)S(1)} collective-permute-done((bf16[16,96,128]{2,1,0:T(8,128)(2,1)}, bf16[16,96,128]{2,1,0:T(8,128)(2,1)S(1)}, u32[]{:S(2)}, u32[]{:S(2)}) %collective-permute-start.5) | collective-permute-done | bytes 393248 | tf_op jit(solution)/shard_map/ppermute | solution.py:582
  94.0 1.0 copy-done.4
  95.8 0.8 copy-done.2
  96.6 1.5 %all-to-all-done.upper_ref = bf16[16,304,128]{2,1,0:T(8,128)(2,1)S(1)} async-done(((bf16[16,304,128]{2,1,0:T(8,128)(2,1)}), bf16[16,304,128]{2,1,0:T(8,128)(2,1)S(1)}, u32[]{:S(2)}, u32[]{:S(2)}) %all-to-all-start) | async-done | bytes 1245216 | tf_op jit(solution)/shard_map/all_to_all | solution.py:611
  98.1 14.4 %all_to_all.15.lower_ref = bf16[16,112,128]{2,1,0:T(8,128)(2,1)S(1)} all-to-all(bf16[16,112,128]{2,1,0:T(8,128)(2,1)} %copy-done.2), channel_id=1, replica_groups=mesh['z'=8,'ylo'=2,'x'=4,'yhi'=2,'core'=2] {'ylo','x','yhi'}, dimensions={0} | all-to-all | bytes 917504 | tf_op jit(solution)/shard_map/all_to_all | solution.py:615
  112.5 1.4 shard_map.213
  113.9 21.2 %all_to_all.16.got_ref = bf16[8,176,128]{2,1,0:T(8,128)(2,1)S(1)} all-to-all(bf16[8,176,128]{2,1,0:T(8,128)(2,1)S(1)} %shard_map.213), channel_id=1, replica_groups=mesh['z'=8,'ylo'=2,'x'=4,'yhi'=2,'core'=2] {'z'}, dimensions={0} | all-to-all | bytes 720896 | tf_op jit(solution)/shard_map/all_to_all | solution.py:616
  135.7 4.4 %collective-permute-start.6 = (f32[104,128]{1,0:T(8,128)S(1)}, f32[104,128]{1,0:T(8,128)S(1)}, u32[]{:S(2)}, u32[]{:S(2)}) collective-permute-start(f32[104,128]{1,0:T(8,128)S(1)} %get-tuple-element.75), channel_id=1, source_target_pairs={{0,1},{1,0},{2,3},{3,2},{4,5},{5,4},{6,7},{7,6},{8,9},{9,8},{10,11... | collective-permute-start | bytes 159752 | tf_op jit(solution)/shard_map/ppermute | solution.py:582
  140.2 0.9 collective-permute-done.6.got_ref
  141.0 1.2 shard_map.215
  (39 shorter events, 3.3 us)
Async XLA Ops:
  0.6 20.4 %copy-start = (bf16[1024,1024]{1,0:T(8,128)(2,1)S(1)}, bf16[1024,1024]{1,0:T(8,128)(2,1)}, u32[]{:S(2)}) copy-start(bf16[1024,1024]{1,0:T(8,128)(2,1)} %param.30) | copy-start | bytes 6291460
  1.6 15.9 %copy-start.12 = (bf16[3,1024]{1,0:T(4,128)(2,1)S(1)}, bf16[3,1024]{1,0:T(4,128)(2,1)}, u32[]{:S(2)}) copy-start(bf16[3,1024]{1,0:T(4,128)(2,1)} %param.20) | copy-start | bytes 18436
  1.6 16.0 %copy-start.10 = (bf16[1024,512]{1,0:T(8,128)(2,1)S(1)}, bf16[1024,512]{1,0:T(8,128)(2,1)}, u32[]{:S(2)}) copy-start(bf16[1024,512]{1,0:T(8,128)(2,1)} %param.24) | copy-start | bytes 3145732
  3.1 17.2 %copy-start.13 = (s32[3,2]{0,1:T(2,128)S(1)}, s32[3,2]{0,1:T(2,128)}, u32[]{:S(2)}) copy-start(s32[3,2]{0,1:T(2,128)} %param.21) | copy-start | bytes 76
  3.9 18.1 %collective-permute-start.1 = (bf16[272,512]{1,0:T(8,128)(2,1)}, bf16[272,512]{1,0:T(8,128)(2,1)}, u32[]{:S(2)}, u32[]{:S(2)}) collective-permute-start(bf16[272,512]{1,0:T(8,128)(2,1)} %pad_maximum_fusion.2), channel_id=1, source_target_pairs={{0,2},{2,0},{3,1},{4,6},{6,4},{7,5},{8,10},{10,8},{11,9},{12,14},{... | collective-permute-start | bytes 835592 | tf_op jit(solution)/shard_map/ppermute | solution.py:577
  5.9 16.1 %collective-permute-start = (bf16[272,512]{1,0:T(8,128)(2,1)}, bf16[272,512]{1,0:T(8,128)(2,1)}, u32[]{:S(2)}, u32[]{:S(2)}) collective-permute-start(bf16[272,512]{1,0:T(8,128)(2,1)} %pad_maximum_fusion.1), channel_id=1, source_target_pairs={{0,1},{1,2},{3,0},{4,5},{5,6},{7,4},{8,9},{9,10},{11,8},{12,13},{1... | collective-permute-start | bytes 835592 | tf_op jit(solution)/shard_map/ppermute | solution.py:577
  15.6 9.7 %collective-permute-start.2 = (bf16[272,512]{1,0:T(8,128)(2,1)}, bf16[272,512]{1,0:T(8,128)(2,1)}, u32[]{:S(2)}, u32[]{:S(2)}) collective-permute-start(bf16[272,512]{1,0:T(8,128)(2,1)} %pad_maximum_fusion.3), channel_id=1, source_target_pairs={{1,0},{2,1},{3,2},{5,4},{6,5},{7,6},{9,8},{10,9},{11,10},{13,12},{... | collective-permute-start | bytes 835592 | tf_op jit(solution)/shard_map/ppermute | solution.py:577
  17.5 7.7 %copy-start.11 = (bf16[1,1024]{1,0:T(2,128)(2,1)}, bf16[1,1024]{1,0:T(2,128)(2,1)S(1)}, u32[]{:S(2)}) copy-start(bf16[1,1024]{1,0:T(2,128)(2,1)S(1)} %constant_dynamic-slice_fusion.dense_ref) | copy-start | bytes 6148
  40.5 20.8 %collective-permute-start.3 = (bf16[16,192,128]{2,1,0:T(8,128)(2,1)}, bf16[16,192,128]{2,1,0:T(8,128)(2,1)S(1)}, u32[]{:S(2)}, u32[]{:S(2)}) collective-permute-start(bf16[16,192,128]{2,1,0:T(8,128)(2,1)} %get-tuple-element.46), channel_id=1, source_target_pairs={{0,1},{1,0},{2,3},{3,2},{4,5},{5,4},{6,7},{7,6},{8,9},{9,8},{10,11... | collective-permute-start | bytes 2359304 | tf_op jit(solution)/shard_map/ppermute | solution.py:582
  54.1 15.7 %copy-start.3 = (bf16[16,192,128]{2,1,0:T(8,128)(2,1)S(1)}, bf16[16,192,128]{2,1,0:T(8,128)(2,1)}, u32[]{:S(2)}) copy-start(bf16[16,192,128]{2,1,0:T(8,128)(2,1)} %get-tuple-element.45.refs_0_) | copy-start | bytes 2359300
  54.1 15.7 %copy-start.9 = (bf16[16,128]{1,0:T(8,128)(2,1)S(1)}, bf16[16,128]{1,0:T(8,128)(2,1)}, u32[]{:S(2)}) copy-start(bf16[16,128]{1,0:T(8,128)(2,1)} %get-tuple-element.44.packet_ref) | copy-start | bytes 12292
  61.3 8.6 %collective-permute-start.4 = (bf16[16,96,128]{2,1,0:T(8,128)(2,1)}, bf16[16,96,128]{2,1,0:T(8,128)(2,1)S(1)}, u32[]{:S(2)}, u32[]{:S(2)}) collective-permute-start(bf16[16,96,128]{2,1,0:T(8,128)(2,1)} %get-tuple-element.59), channel_id=1, source_target_pairs={{0,1},{1,0},{2,3},{3,2},{4,5},{5,4},{6,7},{7,6},{8,9},{9,8},{10,11... | collective-permute-start | bytes 1179656 | tf_op jit(solution)/shard_map/ppermute | solution.py:582
  69.8 1.0 copy-start.5
  71.1 1.0 copy-start.1
  72.2 26.0 %all-to-all-start = ((bf16[16,304,128]{2,1,0:T(8,128)(2,1)}), bf16[16,304,128]{2,1,0:T(8,128)(2,1)S(1)}, u32[]{:S(2)}, u32[]{:S(2)}) async-start(bf16[16,304,128]{2,1,0:T(8,128)(2,1)} %copy-done.1), calls=%async_computation | async-start | bytes 2490368 | tf_op jit(solution)/shard_map/all_to_all | solution.py:611
  77.9 34.6 %copy-start.6 = (f32[1024,2]{0,1:T(2,128)S(1)}, f32[1024,2]{0,1:T(2,128)}, u32[]{:S(2)}) copy-start(f32[1024,2]{0,1:T(2,128)} %param.32) | copy-start | bytes 24580
  85.1 27.4 %copy-start.7 = (s32[8]{0:T(128)S(1)}, s32[8]{0:T(128)}, u32[]{:S(2)}) copy-start(s32[8]{0:T(128)} %fusion.12.meta) | copy-start | bytes 100
  85.1 9.0 %collective-permute-start.5 = (bf16[16,96,128]{2,1,0:T(8,128)(2,1)}, bf16[16,96,128]{2,1,0:T(8,128)(2,1)S(1)}, u32[]{:S(2)}, u32[]{:S(2)}) collective-permute-start(bf16[16,96,128]{2,1,0:T(8,128)(2,1)} %get-tuple-element.71), channel_id=1, source_target_pairs={{0,1},{1,0},{2,3},{3,2},{4,5},{5,4},{6,7},{7,6},{8,9},{9,8},{10,11... | collective-permute-start | bytes 1179656 | tf_op jit(solution)/shard_map/ppermute | solution.py:582
  94.0 1.0 copy-start.4
  95.0 0.7 copy-start.8
  95.8 0.8 copy-start.2
  135.7 5.3 %collective-permute-start.6 = (f32[104,128]{1,0:T(8,128)S(1)}, f32[104,128]{1,0:T(8,128)S(1)}, u32[]{:S(2)}, u32[]{:S(2)}) collective-permute-start(f32[104,128]{1,0:T(8,128)S(1)} %get-tuple-element.75), channel_id=1, source_target_pairs={{0,1},{1,0},{2,3},{3,2},{4,5},{5,4},{6,7},{7,6},{8,9},{9,8},{10,11... | collective-permute-start | bytes 159752 | tf_op jit(solution)/shard_map/ppermute | solution.py:582

commit v4 on v3

--- a/solution.py
+++ b/solution.py
@@ -85,7 +85,7 @@
 
     @pl.when(step == 0)
     def _():
-        for copy in copies:
+        for copy in copies[:4]:
             copy.start()
         sum_ref[...] = jnp.zeros_like(sum_ref)
         term_acc[...] = jnp.zeros_like(term_acc)
@@ -99,19 +99,23 @@
 
     def ahead(c):
         here = slice(c * BLOCK, (c + 1) * BLOCK)
-        if c == 0:
-            for copy in copies[:4]:
-                copy.wait()
         codes = part_ref[BLOCK:, :].astype(F32)
         ids = (codes[:, :BLOCK] * 256.0 + codes[:, BLOCK:]).T[:, 0:1].astype(jnp.int32)
         slots = lax.broadcasted_iota(jnp.int32, (BLOCK, VOCAB), 1)
         picked = jnp.where(slots == ids, 1.0, 0.0).astype(BF16)
+        if c == 0:
+            copies[0].wait()
+            for copy in copies[4:]:
+                copy.start()
         tokens = dot(picked, table_ref[...]) + part_ref[:BLOCK, :].astype(F32)
         mean = jnp.mean(tokens * tokens, axis=1, keepdims=True)
         normed = tokens * lax.rsqrt(mean + EPSILON)
         normed_ref[...] = normed.astype(BF16)
         mixed = (normed * gain_ref[...] + mix_ref[...]).astype(BF16)
         mixed_ref[...] = mixed
+        if c == 0:
+            for copy in copies[1:4]:
+                copy.wait()
         queries = (dot(mixed, wq_ref[...]).astype(BF16).astype(F32) * 0.125).astype(BF16)
         q_ref[...] = queries
         q_all[...] = queries
@@ -161,6 +165,8 @@
 
     def blank(c):
         if c == 0:
+            for copy in copies[4:]:
+                copy.start()
             for copy in copies:
                 copy.wait()
         here = slice(c * BLOCK, (c + 1) * BLOCK)

time: 143 us -> 142 us (level)
  blocking collectives: 35.6 us -> 33.6 us
    all_to_all x1, blocking collectives: 21.2 us -> 19.1 us  [per_device(): lax.all_to_all(sum_pieces(meta, upper_plane, lower_plane, heads), 'z', 0, 0)]
    all_to_all x1, starting transfers between devices: 5.76 us -> 7.3 us  [per_device(): upper_plane = lax.all_to_all(pieces, PLANE, 0, 0)]
where the time goes in v4:
time: 142 us; the launch traced here: 141 us
  starting transfers between devices  51.7 us (36%)
  blocking collectives  33.6 us (24%)
  Pallas kernels  32.6 us (23%)
  waiting for transfers between devices  8.66 us (6%)
  local copies, waits for them, and re-layouts  7.98 us (6%)
  other arithmetic  3.77 us (3%)
  matrix products  1.81 us (1%)
    ppermute x4, starting transfers between devices, swap_cores(): return lax.ppermute(value, 'core', [(0, 1), (1, 0)])  32.3 us
    all_to_all x1, blocking collectives, per_device(): lax.all_to_all(sum_pieces(meta, upper_plane, lower_plane, heads), 'z', 0, 0)  19.1 us
    pallas_call x1, Pallas kernels, forward(): pl.pallas_call(forward_kernel, grid_spec=pltpu.PrefetchScalarGridSpec(num...  14.8 us
    all_to_all x1, blocking collectives, per_device(): lower_plane = lax.all_to_all(pieces, PLANE, 0, 0)  14.5 us
    pallas_call x2, Pallas kernels, pairs_back(): pl.pallas_call(functools.partial(pairs_kernel, first), grid_spec=pltpu.Pr...  14.2 us
    ppermute x3, starting transfers between devices, to_samples(): got.append(lax.ppermute(part((me + k) % 4), CTX, pairs))  12.1 us
    all_to_all x1, starting transfers between devices, per_device(): upper_plane = lax.all_to_all(pieces, PLANE, 0, 0)  7.3 us
    unnamed x33, local copies, waits for them, and re-layouts  5.22 us
  transfers between devices with their start and end apart: 8, of which 5 were waited for; matrix products, arithmetic and copies ran while one was open for 4% of the time, Pallas kernels for 10%

profile of v4, /device:TPU:1, one launch (start us, length us, event | category | flops | bytes accessed | tf_op | source)
XLA Modules:
  0.0 141.3 jit_solution(17188829815970650143)
XLA Ops:
  0.7 0.8 fusion.11
  1.8 1.4 dynamic-slice_bitcast_fusion
  3.9 1.3 collective-permute-start.1
  5.2 0.7 pad_maximum_fusion.1
  5.9 8.9 %collective-permute-start = (bf16[272,512]{1,0:T(8,128)(2,1)}, bf16[272,512]{1,0:T(8,128)(2,1)}, u32[]{:S(2)}, u32[]{:S(2)}) collective-permute-start(bf16[272,512]{1,0:T(8,128)(2,1)} %pad_maximum_fusion.1), channel_id=1, source_target_pairs={{0,1},{1,2},{3,0},{4,5},{5,6},{7,4},{8,9},{9,10},{11,8},{12,13},{1... | collective-permute-start | bytes 835592 | tf_op jit(solution)/shard_map/ppermute | solution.py:583
  14.8 0.7 pad_maximum_fusion.3
  15.6 1.9 %collective-permute-start.2 = (bf16[272,512]{1,0:T(8,128)(2,1)}, bf16[272,512]{1,0:T(8,128)(2,1)}, u32[]{:S(2)}, u32[]{:S(2)}) collective-permute-start(bf16[272,512]{1,0:T(8,128)(2,1)} %pad_maximum_fusion.3), channel_id=1, source_target_pairs={{1,0},{2,1},{3,2},{5,4},{6,5},{7,6},{9,8},{10,9},{11,10},{13,12},{... | collective-permute-start | bytes 835592 | tf_op jit(solution)/shard_map/ppermute | solution.py:583
  17.6 0.8 fusion.7.mix_ref
  18.4 0.7 pad_maximum_fusion.part0
  19.1 1.2 fusion.12.meta
  21.0 1.0 fusion.5.base_ref
  22.0 3.2 %collective-permute-done.2.part3 = bf16[272,512]{1,0:T(8,128)(2,1)} collective-permute-done((bf16[272,512]{1,0:T(8,128)(2,1)}, bf16[272,512]{1,0:T(8,128)(2,1)}, u32[]{:S(2)}, u32[]{:S(2)}) %collective-permute-start.2) | collective-permute-done | bytes 278560 | tf_op jit(solution)/shard_map/ppermute | solution.py:583
  25.2 14.8 %shard_map.208 = (bf16[1024,512]{1,0:T(8,128)(2,1)}, bf16[1024,512]{1,0:T(8,128)(2,1)}, bf16[1024,512]{1,0:T(8,128)(2,1)}, bf16[1024,512]{1,0:T(8,128)(2,1)}, bf...) custom-call(s32[8]{0:T(128)} %fusion.12.meta, ...), custom_call_target="tpu_custom_call" | custom-call | flops 10000000000 | bytes 20000000 | tf_op jit(solution)/shard_map/pallas_call | solution.py:457
  40.0 13.6 %collective-permute-start.3 = (bf16[16,192,128]{2,1,0:T(8,128)(2,1)}, bf16[16,192,128]{2,1,0:T(8,128)(2,1)S(1)}, u32[]{:S(2)}, u32[]{:S(2)}) collective-permute-start(bf16[16,192,128]{2,1,0:T(8,128)(2,1)} %get-tuple-element.46), channel_id=1, source_target_pairs={{0,1},{1,0},{2,3},{3,2},{4,5},{5,4},{6,7},{7,6},{8,9},{9,8},{10,11... | collective-permute-start | bytes 2359304 | tf_op jit(solution)/shard_map/ppermute | solution.py:588
  53.7 7.1 %shard_map.209 = (bf16[16,96,128]{2,1,0:T(8,128)(2,1)}, bf16[16,96,128]{2,1,0:T(8,128)(2,1)}, f32[2,512]{1,0:T(2,128)}, bf16[16,128]{1,0:T(8,128)(2,1)}) custom-call(s32[8]{0:T(128)} %fusion.12.meta, s32[3]{0:T(128)} %lengths.5, bf16[1024,512]{1,0:T(8,128)(2,1)} %get-tuple-element.61.q_ref, bf16[1024,512]{1,0:T(8,128)(2,1)} %get-tuple-element.62.k_ref, ...), custom_call_target="tpu_custom_call" | custom-call | flops 10000000000 | bytes 10000000 | tf_op jit(solution)/shard_map/pallas_call | solution.py:489
  60.8 7.0 %collective-permute-start.4 = (bf16[16,96,128]{2,1,0:T(8,128)(2,1)}, bf16[16,96,128]{2,1,0:T(8,128)(2,1)S(1)}, u32[]{:S(2)}, u32[]{:S(2)}) collective-permute-start(bf16[16,96,128]{2,1,0:T(8,128)(2,1)} %get-tuple-element.59), channel_id=1, source_target_pairs={{0,1},{1,0},{2,3},{3,2},{4,5},{5,4},{6,7},{7,6},{8,9},{9,8},{10,11... | collective-permute-start | bytes 1179656 | tf_op jit(solution)/shard_map/ppermute | solution.py:588
  67.8 1.6 %collective-permute-done.4.refs_3_ = bf16[16,96,128]{2,1,0:T(8,128)(2,1)S(1)} collective-permute-done((bf16[16,96,128]{2,1,0:T(8,128)(2,1)}, bf16[16,96,128]{2,1,0:T(8,128)(2,1)S(1)}, u32[]{:S(2)}, u32[]{:S(2)}) %collective-permute-start.4) | collective-permute-done | bytes 393248 | tf_op jit(solution)/shard_map/ppermute | solution.py:588
  69.4 1.0 copy-done.5
  70.7 1.0 copy-done.1
  71.7 7.3 %all-to-all-start = ((bf16[16,304,128]{2,1,0:T(8,128)(2,1)}), bf16[16,304,128]{2,1,0:T(8,128)(2,1)S(1)}, u32[]{:S(2)}, u32[]{:S(2)}) async-start(bf16[16,304,128]{2,1,0:T(8,128)(2,1)} %copy-done.1), calls=%async_computation | async-start | bytes 2490368 | tf_op jit(solution)/shard_map/all_to_all | solution.py:617
  79.0 7.1 %shard_map.211 = (bf16[16,96,128]{2,1,0:T(8,128)(2,1)}, bf16[16,96,128]{2,1,0:T(8,128)(2,1)}, f32[2,512]{1,0:T(2,128)}, bf16[16,128]{1,0:T(8,128)(2,1)}) custom-call(s32[8]{0:T(128)} %fusion.12.meta, s32[3]{0:T(128)} %lengths.5, bf16[1024,512]{1,0:T(8,128)(2,1)} %get-tuple-element.61.q_ref, bf16[1024,512]{1,0:T(8,128)(2,1)} %get-tuple-element.62.k_ref, ...), custom_call_target="tpu_custom_call" | custom-call | flops 10000000000 | bytes 10000000 | tf_op jit(solution)/shard_map/pallas_call | solution.py:489
  86.1 7.4 %collective-permute-start.5 = (bf16[16,96,128]{2,1,0:T(8,128)(2,1)}, bf16[16,96,128]{2,1,0:T(8,128)(2,1)S(1)}, u32[]{:S(2)}, u32[]{:S(2)}) collective-permute-start(bf16[16,96,128]{2,1,0:T(8,128)(2,1)} %get-tuple-element.71), channel_id=1, source_target_pairs={{0,1},{1,0},{2,3},{3,2},{4,5},{5,4},{6,7},{7,6},{8,9},{9,8},{10,11... | collective-permute-start | bytes 1179656 | tf_op jit(solution)/shard_map/ppermute | solution.py:588
  93.5 1.6 %collective-permute-done.5.refs_1_ = bf16[16,96,128]{2,1,0:T(8,128)(2,1)S(1)} collective-permute-done((bf16[16,96,128]{2,1,0:T(8,128)(2,1)}, bf16[16,96,128]{2,1,0:T(8,128)(2,1)S(1)}, u32[]{:S(2)}, u32[]{:S(2)}) %collective-permute-start.5) | collective-permute-done | bytes 393248 | tf_op jit(solution)/shard_map/ppermute | solution.py:588
  95.1 1.0 copy-done.4
  96.9 0.8 copy-done.2
  97.7 1.4 %all-to-all-done.upper_ref = bf16[16,304,128]{2,1,0:T(8,128)(2,1)S(1)} async-done(((bf16[16,304,128]{2,1,0:T(8,128)(2,1)}), bf16[16,304,128]{2,1,0:T(8,128)(2,1)S(1)}, u32[]{:S(2)}, u32[]{:S(2)}) %all-to-all-start) | async-done | bytes 1245216 | tf_op jit(solution)/shard_map/all_to_all | solution.py:617
  99.1 14.5 %all_to_all.15.lower_ref = bf16[16,112,128]{2,1,0:T(8,128)(2,1)S(1)} all-to-all(bf16[16,112,128]{2,1,0:T(8,128)(2,1)} %copy-done.2), channel_id=1, replica_groups=mesh['z'=8,'ylo'=2,'x'=4,'yhi'=2,'core'=2] {'ylo','x','yhi'}, dimensions={0} | all-to-all | bytes 917504 | tf_op jit(solution)/shard_map/all_to_all | solution.py:621
  113.6 1.4 shard_map.213
  115.0 19.1 %all_to_all.16.got_ref = bf16[8,176,128]{2,1,0:T(8,128)(2,1)S(1)} all-to-all(bf16[8,176,128]{2,1,0:T(8,128)(2,1)S(1)} %shard_map.213), channel_id=1, replica_groups=mesh['z'=8,'ylo'=2,'x'=4,'yhi'=2,'core'=2] {'z'}, dimensions={0} | all-to-all | bytes 720896 | tf_op jit(solution)/shard_map/all_to_all | solution.py:622
  134.7 4.3 %collective-permute-start.6 = (f32[104,128]{1,0:T(8,128)S(1)}, f32[104,128]{1,0:T(8,128)S(1)}, u32[]{:S(2)}, u32[]{:S(2)}) collective-permute-start(f32[104,128]{1,0:T(8,128)S(1)} %get-tuple-element.75), channel_id=1, source_target_pairs={{0,1},{1,0},{2,3},{3,2},{4,5},{5,4},{6,7},{7,6},{8,9},{9,8},{10,11... | collective-permute-start | bytes 159752 | tf_op jit(solution)/shard_map/ppermute | solution.py:588
  138.9 0.9 collective-permute-done.6.got_ref
  139.8 1.2 shard_map.215
  (39 shorter events, 3.3 us)
Async XLA Ops:
  0.6 20.4 %copy-start = (bf16[1024,1024]{1,0:T(8,128)(2,1)S(1)}, bf16[1024,1024]{1,0:T(8,128)(2,1)}, u32[]{:S(2)}) copy-start(bf16[1024,1024]{1,0:T(8,128)(2,1)} %param.30) | copy-start | bytes 6291460
  1.6 15.9 %copy-start.12 = (bf16[3,1024]{1,0:T(4,128)(2,1)S(1)}, bf16[3,1024]{1,0:T(4,128)(2,1)}, u32[]{:S(2)}) copy-start(bf16[3,1024]{1,0:T(4,128)(2,1)} %param.20) | copy-start | bytes 18436
  1.6 16.0 %copy-start.10 = (bf16[1024,512]{1,0:T(8,128)(2,1)S(1)}, bf16[1024,512]{1,0:T(8,128)(2,1)}, u32[]{:S(2)}) copy-start(bf16[1024,512]{1,0:T(8,128)(2,1)} %param.24) | copy-start | bytes 3145732
  3.1 17.2 %copy-start.13 = (s32[3,2]{0,1:T(2,128)S(1)}, s32[3,2]{0,1:T(2,128)}, u32[]{:S(2)}) copy-start(s32[3,2]{0,1:T(2,128)} %param.21) | copy-start | bytes 76
  3.9 18.1 %collective-permute-start.1 = (bf16[272,512]{1,0:T(8,128)(2,1)}, bf16[272,512]{1,0:T(8,128)(2,1)}, u32[]{:S(2)}, u32[]{:S(2)}) collective-permute-start(bf16[272,512]{1,0:T(8,128)(2,1)} %pad_maximum_fusion.2), channel_id=1, source_target_pairs={{0,2},{2,0},{3,1},{4,6},{6,4},{7,5},{8,10},{10,8},{11,9},{12,14},{... | collective-permute-start | bytes 835592 | tf_op jit(solution)/shard_map/ppermute | solution.py:583
  5.9 16.1 %collective-permute-start = (bf16[272,512]{1,0:T(8,128)(2,1)}, bf16[272,512]{1,0:T(8,128)(2,1)}, u32[]{:S(2)}, u32[]{:S(2)}) collective-permute-start(bf16[272,512]{1,0:T(8,128)(2,1)} %pad_maximum_fusion.1), channel_id=1, source_target_pairs={{0,1},{1,2},{3,0},{4,5},{5,6},{7,4},{8,9},{9,10},{11,8},{12,13},{1... | collective-permute-start | bytes 835592 | tf_op jit(solution)/shard_map/ppermute | solution.py:583
  15.6 9.7 %collective-permute-start.2 = (bf16[272,512]{1,0:T(8,128)(2,1)}, bf16[272,512]{1,0:T(8,128)(2,1)}, u32[]{:S(2)}, u32[]{:S(2)}) collective-permute-start(bf16[272,512]{1,0:T(8,128)(2,1)} %pad_maximum_fusion.3), channel_id=1, source_target_pairs={{1,0},{2,1},{3,2},{5,4},{6,5},{7,6},{9,8},{10,9},{11,10},{13,12},{... | collective-permute-start | bytes 835592 | tf_op jit(solution)/shard_map/ppermute | solution.py:583
  17.5 7.7 %copy-start.11 = (bf16[1,1024]{1,0:T(2,128)(2,1)}, bf16[1,1024]{1,0:T(2,128)(2,1)S(1)}, u32[]{:S(2)}) copy-start(bf16[1,1024]{1,0:T(2,128)(2,1)S(1)} %constant_dynamic-slice_fusion.dense_ref) | copy-start | bytes 6148
  40.0 20.8 %collective-permute-start.3 = (bf16[16,192,128]{2,1,0:T(8,128)(2,1)}, bf16[16,192,128]{2,1,0:T(8,128)(2,1)S(1)}, u32[]{:S(2)}, u32[]{:S(2)}) collective-permute-start(bf16[16,192,128]{2,1,0:T(8,128)(2,1)} %get-tuple-element.46), channel_id=1, source_target_pairs={{0,1},{1,0},{2,3},{3,2},{4,5},{5,4},{6,7},{7,6},{8,9},{9,8},{10,11... | collective-permute-start | bytes 2359304 | tf_op jit(solution)/shard_map/ppermute | solution.py:588
  53.7 15.7 %copy-start.3 = (bf16[16,192,128]{2,1,0:T(8,128)(2,1)S(1)}, bf16[16,192,128]{2,1,0:T(8,128)(2,1)}, u32[]{:S(2)}) copy-start(bf16[16,192,128]{2,1,0:T(8,128)(2,1)} %get-tuple-element.45.refs_0_) | copy-start | bytes 2359300
  53.7 15.7 %copy-start.9 = (bf16[16,128]{1,0:T(8,128)(2,1)S(1)}, bf16[16,128]{1,0:T(8,128)(2,1)}, u32[]{:S(2)}) copy-start(bf16[16,128]{1,0:T(8,128)(2,1)} %get-tuple-element.44.packet_ref) | copy-start | bytes 12292
  60.8 8.6 %collective-permute-start.4 = (bf16[16,96,128]{2,1,0:T(8,128)(2,1)}, bf16[16,96,128]{2,1,0:T(8,128)(2,1)S(1)}, u32[]{:S(2)}, u32[]{:S(2)}) collective-permute-start(bf16[16,96,128]{2,1,0:T(8,128)(2,1)} %get-tuple-element.59), channel_id=1, source_target_pairs={{0,1},{1,0},{2,3},{3,2},{4,5},{5,4},{6,7},{7,6},{8,9},{9,8},{10,11... | collective-permute-start | bytes 1179656 | tf_op jit(solution)/shard_map/ppermute | solution.py:588
  69.4 1.0 copy-start.5
  70.6 1.0 copy-start.1
  71.7 27.4 %all-to-all-start = ((bf16[16,304,128]{2,1,0:T(8,128)(2,1)}), bf16[16,304,128]{2,1,0:T(8,128)(2,1)S(1)}, u32[]{:S(2)}, u32[]{:S(2)}) async-start(bf16[16,304,128]{2,1,0:T(8,128)(2,1)} %copy-done.1), calls=%async_computation | async-start | bytes 2490368 | tf_op jit(solution)/shard_map/all_to_all | solution.py:617
  79.0 34.6 %copy-start.6 = (f32[1024,2]{0,1:T(2,128)S(1)}, f32[1024,2]{0,1:T(2,128)}, u32[]{:S(2)}) copy-start(f32[1024,2]{0,1:T(2,128)} %param.32) | copy-start | bytes 24580
  86.1 27.5 %copy-start.7 = (s32[8]{0:T(128)S(1)}, s32[8]{0:T(128)}, u32[]{:S(2)}) copy-start(s32[8]{0:T(128)} %fusion.12.meta) | copy-start | bytes 100
  86.1 9.0 %collective-permute-start.5 = (bf16[16,96,128]{2,1,0:T(8,128)(2,1)}, bf16[16,96,128]{2,1,0:T(8,128)(2,1)S(1)}, u32[]{:S(2)}, u32[]{:S(2)}) collective-permute-start(bf16[16,96,128]{2,1,0:T(8,128)(2,1)} %get-tuple-element.71), channel_id=1, source_target_pairs={{0,1},{1,0},{2,3},{3,2},{4,5},{5,4},{6,7},{7,6},{8,9},{9,8},{10,11... | collective-permute-start | bytes 1179656 | tf_op jit(solution)/shard_map/ppermute | solution.py:588
  95.1 1.0 copy-start.4
  96.1 0.7 copy-start.8
  96.9 0.8 copy-start.2
  134.7 5.1 %collective-permute-start.6 = (f32[104,128]{1,0:T(8,128)S(1)}, f32[104,128]{1,0:T(8,128)S(1)}, u32[]{:S(2)}, u32[]{:S(2)}) collective-permute-start(f32[104,128]{1,0:T(8,128)S(1)} %get-tuple-element.75), channel_id=1, source_target_pairs={{0,1},{1,0},{2,3},{3,2},{4,5},{5,4},{6,7},{7,6},{8,9},{9,8},{10,11... | collective-permute-start | bytes 159752 | tf_op jit(solution)/shard_map/ppermute | solution.py:588
